TPU v7x, 128 devices: a whole 4x4x4 slice. The times are simulated.
128 devices in a mesh: chan: 16 (over z, x_hi, core), sect: 8 (over x_lo, y).
Axes of the slice: x: 4 (x_hi: 2, x_lo: 2; x = x_hi * 2 + x_lo), y: 4, z: 4, core: 2. Of those that a mesh axis runs over, the one named last changes fastest.
Arguments:
- voltages: bfloat16 [2, 512, 524288], P(None, 'chan', 'sect'), may hold values from -6 to 6
- fir_taps: float32 [4, 4096], replicated, may hold values from -3 to 3
- station_map: int32 [512], replicated, may hold values from 0 to 511, each once
- band_start: int32 [32], replicated, may hold values from 0 to 4032, as said below
- calib: bfloat16 [2, 2048, 512], P(None, ('chan', 'sect')), may hold values from -6 to 6
- steer: bfloat16 [1024, 2, 512], P('sect'), may hold values from -0.1875 to 0.1875
- beam_index: int32 [500], replicated, may hold values from 0 to 1023
Outputs:
- visibility: float32 [2, 512, 512, 512], P(None, ('chan', 'sect'))
- beams: bfloat16 [2, 2048, 500, 128], P(None, ('chan', 'sect'))
Inputs may be any that keep to these rules, and one draw needn't show every extreme that they name: `band_start`: distinct multiples of 64, so the kept sub-bands never share a channel.
All inputs are finite; a program needn't handle non-finite values.
Results may differ from a plain program's by a relative error of at most 0.02.
Values may be sent and summed in bfloat16 or wider, within the bound.
A program may use at most 192 MiB of HBM per device.

v0:
```python
import math

import jax
import jax.numpy as jnp
from jax import lax
from jax.sharding import PartitionSpec as P

RADIX = 64
AVG = 4
SUBW = 64


def from_behind(block, axis, distance):
    devices = range(lax.axis_size(axis))
    route = [(i - distance, i) for i in devices if i - distance in devices]
    return lax.ppermute(block, axis, route)


def transform(filtered):
    factor = RADIX
    length = factor * factor
    shape_in = filtered.shape[1:]
    steps_idx = jnp.arange(factor, dtype=jnp.int32)
    outer = steps_idx[:, None] * steps_idx[None, :]
    angle = 2.0 * math.pi / factor * (outer % factor).astype(jnp.float32)
    norm_factor = 1.0 / math.sqrt(factor)
    cosine = jnp.cos(angle) * norm_factor
    sine = jnp.sin(angle) * norm_factor
    table = jnp.stack([jnp.stack([cosine, -sine]), jnp.stack([sine, cosine])]).astype(jnp.bfloat16)
    twist_angle = 2.0 * math.pi / length * outer.astype(jnp.float32)
    twist_cos = jnp.cos(twist_angle)
    twist_sin = jnp.sin(twist_angle)
    grid = filtered.astype(jnp.bfloat16).reshape((2,) + shape_in[:-1] + (factor, factor))
    first = jnp.einsum("csfab,cdak->dsfkb", grid, table, preferred_element_type=jnp.float32)
    real_two = first[0] * twist_cos + first[1] * twist_sin
    imag_two = first[1] * twist_cos - first[0] * twist_sin
    middle = jnp.stack([real_two, imag_two]).astype(jnp.bfloat16)
    second = jnp.einsum("csfkb,cdbm->dsfmk", middle, table, preferred_element_type=jnp.float32)
    return second.reshape((2,) + shape_in)


def correlate(ordered, scale):
    swapped = jnp.stack([ordered[1], -ordered[0]])
    real_vis = jnp.einsum("cmapf,cmaqf->mpq", ordered, ordered, preferred_element_type=jnp.float32)
    imag_vis = jnp.einsum("cmapf,cmaqf->mpq", swapped, ordered, preferred_element_type=jnp.float32)
    return jnp.stack([real_vis, imag_vis]) * scale


def beamform(ordered, calib, weights):
    gain_real = calib[0].astype(jnp.float32)[:, :, None]
    gain_imag = calib[1].astype(jnp.float32)[:, :, None]
    volt_real = ordered[0].astype(jnp.float32)
    volt_imag = ordered[1].astype(jnp.float32)
    cal_real = (gain_real * volt_real - gain_imag * volt_imag).astype(jnp.bfloat16)
    cal_imag = (gain_real * volt_imag + gain_imag * volt_real).astype(jnp.bfloat16)
    first_pair = jnp.stack([cal_real, -cal_imag])
    second_pair = jnp.stack([cal_imag, cal_real])
    real_beam = jnp.einsum("bcp,cjpf->jbf", weights, first_pair, preferred_element_type=jnp.float32)
    imag_beam = jnp.einsum(
        "bcp,cjpf->jbf", weights, second_pair, preferred_element_type=jnp.float32
    )
    return jnp.stack([real_beam, imag_beam]).astype(jnp.bfloat16)


def shards(voltages, fir_taps, station_map, band_start, calib, steer, beam_index):
    chan_count = lax.axis_size("chan")
    sect_count = lax.axis_size("sect")
    device_count = chan_count * sect_count
    stations_here = voltages.shape[1]
    taps_count = fir_taps.shape[0]
    length = fir_taps.shape[1]
    frames_here = voltages.shape[2] // length
    station_total = stations_here * chan_count
    frame_total = frames_here * sect_count
    blocks = voltages.reshape(2, stations_here, frames_here, length)
    tail = blocks[:, :, frames_here - (taps_count - 1) :]
    earlier = from_behind(tail, "sect", 1)
    extended = jnp.concatenate([earlier, blocks], axis=2)
    filtered = jnp.zeros((2, stations_here, frames_here, length), jnp.float32)
    for tap_index in range(taps_count):
        window = extended[
            :, :, taps_count - 1 - tap_index : taps_count - 1 - tap_index + frames_here
        ]
        filtered = filtered + fir_taps[tap_index][None, None, None, :] * window.astype(jnp.float32)
    spectra = transform(filtered)
    band_slots = band_start // SUBW
    slot_total = length // SUBW
    picked = jnp.take(
        spectra.reshape(2, stations_here, frames_here, slot_total, SUBW), band_slots, axis=3
    )
    picked = picked.reshape(2, stations_here, frames_here, -1).astype(jnp.bfloat16)
    outgoing = jnp.transpose(picked, (0, 3, 1, 2))
    kept_total = outgoing.shape[1]
    ch_here = kept_total // device_count
    vis_here = ch_here // AVG
    table = lax.all_gather(steer, "sect", axis=0, tiled=True)
    weights = jnp.take(table, beam_index, axis=0)
    inverse = (
        jnp.zeros_like(station_map)
        .at[station_map]
        .set(jnp.arange(station_map.shape[0], dtype=jnp.int32))
    )
    scale = 1.0 / (AVG * frame_total)
    sending = outgoing.reshape(2, device_count, vis_here, AVG, stations_here, frames_here)
    received = lax.all_to_all(sending, ("chan", "sect"), split_axis=1, concat_axis=1, tiled=True)
    items = received.shape[2]
    grid = received.reshape(2, chan_count, sect_count, items, AVG, stations_here, frames_here)
    grid = jnp.transpose(grid, (0, 3, 4, 1, 5, 2, 6))
    grid = grid.reshape(2, items, AVG, station_total, frame_total)
    arranged = jnp.take(grid, inverse, axis=3)
    ordered = arranged.reshape(2, ch_here, station_total, frame_total)
    visibility = correlate(arranged, scale)
    beams = beamform(ordered, calib, weights)
    return (visibility, beams)


def solution(mesh):
    return jax.shard_map(
        shards,
        mesh=mesh,
        in_specs=(
            P(None, "chan", "sect"),
            P(),
            P(),
            P(),
            P(None, ("chan", "sect"), None),
            P("sect", None, None),
            P(),
        ),
        out_specs=(P(None, ("chan", "sect"), None, None), P(None, ("chan", "sect"), None, None)),
        check_vma=False,
    )
```

profile of v0, /device:TPU:4, one launch (start us, length us, event | category | flops | bytes accessed | tf_op | source)
XLA Modules:
  0.0 521.4 jit_solution(16997183366064281419)
XLA Ops:
  7.2 12.1 %copy.110 = bf16[8,8,16,4096]{3,2,1,0:T(8,128)(2,1)} copy(bf16[8,8,16,4096]{3,1,2,0:T(8,128)(2,1)} %bitcast.122) | data formatting | bytes 16777216
  19.3 3.5 slice.68
  22.8 1.1 copy.83
  24.0 3.6 collective-permute-start
  27.6 0.1 broadcast_in_dim.53
  27.7 0.1 broadcast_in_dim.54
  27.7 0.1 fusion.45
  27.9 0.2 negate_convert_fusion
  28.1 0.1 fusion.40
  28.3 32.8 %collective-permute-done = bf16[2,32,3,4096]{3,1,2,0:T(8,128)(2,1)S(1)} collective-permute-done((bf16[2,32,3,4096]{3,1,2,0:T(8,128)(2,1)S(1)}, bf16[2,32,3,4096]{3,1,2,0:T(8,128)(2,1)S(1)}, u32[]{:S(2)}, u32[]{:S(2)}) %collective-permute-start) | collective-permute-done | bytes 1572896 | tf_op jit(solution)/shard_map/ppermute | solution.py:16
  61.1 1.4 copy.84
  62.4 19.8 %add_convert_fusion.1 = bf16[2,32,16,4096]{3,2,1,0:T(8,128)(2,1)} fusion(bf16[2,32,16,4096]{3,2,1,0:T(8,128)(2,1)} %bitcast.116, bf16[2,32,3,4096]{3,2,1,0:T(4,128)(2,1)S(1)} %copy.84, f32[4096]{0:T(1024)S(1)} %bitcast.125, f32[4096]{0:T(1024)S(1)} %bitcast.126, f32[4096]{0:T(1024)S(1)} %bitcast.124, f32[4096]{0:T(1024)S(1)} %bitcast.123), kind=kLoop, calls=%fused_computation.14 | loop fusion | flops 88080384 | bytes 18415616 | tf_op jit(solution)/shard_map/convert_element_type | solution.py:33
  82.3 23.6 %reshape.237 = bf16[2,32,16,64,64]{4,3,2,1,0:T(8,128)(2,1)} reshape(bf16[2,32,16,4096]{3,2,1,0:T(8,128)(2,1)} %add_convert_fusion.1) | data formatting | bytes 16777216 | tf_op jit(solution)/shard_map/reshape | solution.py:33
  105.9 16.5 %convolution_bitcast_fusion.1 = f32[2,32,16,64,64]{4,3,2,1,0:T(8,128)} fusion(bf16[2,32,16,64,64]{4,3,2,1,0:T(8,128)(2,1)} %reshape.237, bf16[1,2,64,64]{2,3,0,1:T(8,128)(2,1)S(1)} %get-tuple-element.31, bf16[1,2,64,64]{2,3,0,1:T(8,128)(2,1)S(1)} %get-tuple-element.30), kind=kOutput, calls=%fused_computation.5 | convolution fusion | flops 1073807360 | bytes 25198592 | tf_op jit(solution)/shard_map/csfab,cdak->dsfkb/dot_general | solution.py:34
  122.4 15.1 %add_convert_fusion = (bf16[1,32,16,64,64]{4,3,2,1,0:T(8,128)(2,1)S(1)}, bf16[1,32,16,64,64]{4,3,2,1,0:T(8,128)(2,1)}) fusion(f32[2,32,16,64,64]{4,3,2,1,0:T(8,128)} %convolution_bitcast_fusion.1, f32[64,64]{1,0:T(8,128)S(1)} %get-tuple-element.34, f32[64,64]{1,0:T(8,128)S(1)} %get-tuple-element.35), kind=kLoop, calls=%fused_computation.13 | loop fusion | flops 16777216 | bytes 25198592 | tf_op jit(solution)/shard_map/convert.10
  137.4 14.0 %convolution_bitcast_fusion = bf16[2,32,16,64,64]{4,3,2,1,0:T(8,128)(2,1)} fusion(bf16[1,2,64,64]{2,3,0,1:T(8,128)(2,1)S(1)} %get-tuple-element.31, bf16[1,2,64,64]{2,3,0,1:T(8,128)(2,1)S(1)} %get-tuple-element.30, bf16[1,32,16,64,64]{4,3,2,1,0:T(8,128)(2,1)} %get-tuple-element.19, bf16[1,32,16,64,64]{4,3,2,1,0:T(8,128)(2,1)S(1)} %get-tuple-element.18), kind=kOutput, calls=%fused_computation.4 | convolution fusion | flops 1078001664 | bytes 16809984 | tf_op jit(solution)/shard_map/csfkb,cdbm->dsfmk/dot_general | solution.py:38
  151.4 19.7 %copy.87 = bf16[2,32,16,64,64]{4,2,3,1,0:T(8,128)(2,1)} copy(bf16[2,32,16,64,64]{4,3,2,1,0:T(8,128)(2,1)} %convolution_bitcast_fusion) | data formatting | bytes 16777216 | tf_op jit(solution)/shard_map/csfkb,cdbm->dsfmk/transpose | solution.py:38
  171.2 11.7 %gather_fusion = bf16[32,2,32,16,64]{4,3,2,1,0:T(8,128)(2,1)} fusion(bf16[2,32,16,64,64]{4,2,3,1,0:T(8,128)(2,1)} %copy.87, s32[1024]{0:T(1024)S(1)} %pad_clamp_fusion.2), kind=kCustom, calls=%fused_computation | custom fusion | bytes 8388736 | tf_op jit(solution)/shard_map/jit(_take)/gather | solution.py:88
  182.9 16.3 %copy.88 = bf16[2,32,16,32,64]{4,3,2,1,0:T(8,128)(2,1)} copy(bf16[2,32,16,32,64]{4,2,1,0,3:T(8,128)(2,1)} %bitcast.121) | data formatting | bytes 8388608 | tf_op jit(solution)/shard_map/jit(_take)/gather | solution.py:88
  199.2 12.7 %gather.15 = bf16[2,32,16,2048]{3,2,1,0:T(8,128)(2,1)} reshape(bf16[2,32,16,32,64]{4,3,2,1,0:T(8,128)(2,1)} %copy.88) | data formatting | bytes 8388608 | tf_op jit(solution)/shard_map/jit(_take)/gather | solution.py:88
  211.9 5.6 %fusion.6 = bf16[2,2048,32,16]{1,3,2,0:T(8,128)(2,1)} fusion(bf16[2,32,16,2048]{3,2,1,0:T(8,128)(2,1)} %gather.15, pred[2048]{0:T(1024)(128)(4,1)S(1)} %broadcast_in_dim.54), kind=kLoop, calls=%fused_computation.24 | loop fusion | flops 2097152 | bytes 8390656 | tf_op jit(solution)/shard_map/transpose | solution.py:92
  217.5 23.8 %copy.89 = bf16[2,2048,32,16]{2,3,1,0:T(8,128)(2,1)} copy(bf16[2,2048,32,16]{1,3,2,0:T(8,128)(2,1)} %fusion.6) | data formatting | bytes 8388608 | tf_op jit(solution)/shard_map/transpose | solution.py:92
  241.2 15.7 %copy.133 = bf16[2,128,4,4,32,16]{4,5,3,2,0,1:T(8,128)(2,1)} copy(bf16[2,128,4,4,32,16]{4,5,3,2,1,0:T(8,128)(2,1)} %bitcast.111) | data formatting | bytes 8388608 | tf_op jit(solution)/shard_map/reshape | solution.py:104
  256.9 25.0 %reshape.294 = bf16[128,2,8192]{2,1,0:T(2,128)(2,1)} reshape(bf16[128,2,4,4,16,32]{5,4,3,2,1,0:T(8,128)(2,1)} %bitcast.112) | data formatting | bytes 8388608
  281.9 11.9 %all-to-all-start = ((bf16[128,2,8192]{2,1,0:T(2,128)(2,1)}), bf16[128,2,8192]{2,1,0:T(2,128)(2,1)}, u32[]{:S(2)}, u32[]{:S(2)}) async-start(bf16[128,2,8192]{2,1,0:T(2,128)(2,1)} %reshape.294), calls=%async_computation | async-start | bytes 8388608 | tf_op jit(solution)/shard_map/all_to_all | solution.py:105
  293.9 0.7 all-gather.2.cloned.1.call-update
  294.6 2.4 scatter_custom_fusion
  297.1 71.1 %all-gather.2.cloned.1.call-done = bf16[1024,2,512]{2,1,0:T(2,128)(2,1)} async-done(((bf16[128,2,512]{2,1,0:T(2,128)(2,1)}), bf16[1024,2,512]{2,1,0:T(2,128)(2,1)}) %all-gather.2.cloned.1.call-update) | async-done | bytes 2097168 | tf_op jit(solution)/shard_map/all_gather | solution.py:96
  368.2 4.5 gather_fusion.2
  372.7 2.0 broadcast_select_fusion
  374.7 21.9 %reshape.295 = bf16[128,2,4,4,16,32]{5,4,3,2,1,0:T(8,128)(2,1)} reshape(bf16[128,2,8192]{2,1,0:T(2,128)(2,1)} %all-to-all-done) | data formatting | bytes 8388608
  396.6 28.3 %copy.132 = bf16[2,16,8,4,4,32,16]{5,1,6,2,4,3,0:T(8,128)(2,1)} copy(bf16[2,16,8,4,4,32,16]{5,6,4,3,0,2,1:T(8,128)(2,1)} %bitcast.113) | data formatting | bytes 8388608 | tf_op jit(solution)/shard_map/reshape | solution.py:107
  424.9 22.6 %reshape.240 = bf16[2,4,4,512,128]{3,4,2,1,0:T(8,128)(2,1)} reshape(bf16[2,4,4,16,32,8,16]{4,3,6,5,2,1,0:T(8,128)(2,1)} %bitcast.114) | data formatting | bytes 8388608 | tf_op jit(solution)/shard_map/reshape | solution.py:109
  447.5 7.5 %copy.92 = bf16[2,4,4,512,128]{4,2,3,1,0:T(4,128)(2,1)} copy(bf16[2,4,4,512,128]{3,4,2,1,0:T(8,128)(2,1)} %reshape.240) | data formatting | bytes 8388608 | tf_op jit(solution)/shard_map/reshape | solution.py:109
  455.0 28.1 %gather_fusion.1 = bf16[512,2,4,4,128]{4,3,2,1,0:T(4,128)(2,1)} fusion(bf16[2,4,4,512,128]{4,2,3,1,0:T(4,128)(2,1)} %copy.92, s32[1024]{0:T(1024)S(1)} %pad_clamp_fusion.1), kind=kCustom, calls=%fused_computation.1 | custom fusion | bytes 8390656 | tf_op jit(solution)/shard_map/jit(_take)/gather | solution.py:110
  483.1 6.3 %fusion.19 = bf16[2,4,4,512,128]{4,3,0,1,2:T(8,128)(2,1)S(1)} fusion(bf16[512,2,4,4,128]{4,3,2,1,0:T(4,128)(2,1)} %gather_fusion.1, pred[512]{0:T(512)(128)(4,1)S(1)} %compare_and_fusion.2), kind=kLoop, calls=%fused_computation.38 | loop fusion | flops 2097152 | bytes 8389120 | tf_op jit(solution)/shard_map/jit(_take)/select_n | solution.py:110
  489.4 1.8 slice_convert_fusion
  491.2 0.4 copy.94
  491.6 0.4 copy.96
  491.9 2.5 fusion.53
  494.4 2.8 subtract_convert_fusion.1
  497.2 2.4 convolution_bitcast_fusion.2
  499.6 2.4 fusion.27
  501.9 2.3 fusion.30
  504.3 0.4 pad_maximum_fusion.2
  504.7 2.5 copy.102
  507.2 2.4 fusion.20
  509.6 4.5 maximum_multiply_fusion
  (25 shorter events, 0.2 us)
Async XLA Ops:
  19.3 8.2 %copy-start.4 = (s32[32]{0:T(128)S(1)}, s32[32]{0:T(128)}, u32[]{:S(2)}) copy-start(s32[32]{0:T(128)} %param.10) | copy-start | bytes 388
  19.3 8.9 %copy-start = (f32[4,4096]{1,0:T(4,128)S(1)}, f32[4,4096]{1,0:T(4,128)}, u32[]{:S(2)}) copy-start(f32[4,4096]{1,0:T(4,128)} %param.8) | copy-start | bytes 196612
  24.0 37.1 %collective-permute-start = (bf16[2,32,3,4096]{3,1,2,0:T(8,128)(2,1)S(1)}, bf16[2,32,3,4096]{3,1,2,0:T(8,128)(2,1)S(1)}, u32[]{:S(2)}, u32[]{:S(2)}) collective-permute-start(bf16[2,32,3,4096]{3,1,2,0:T(8,128)(2,1)S(1)} %copy.83), channel_id=1, source_target_pairs={{0,1},{1,2},{2,3},{3,4},{4,5},{5,6},{6,7},{8,9},{9,10},{10,11},{11... | collective-permute-start | bytes 4718600 | tf_op jit(solution)/shard_map/ppermute | solution.py:16
  281.9 12.6 %copy-start.3 = (s32[512]{0:T(512)S(1)}, s32[512]{0:T(512)}, u32[]{:S(2)}) copy-start(s32[512]{0:T(512)} %param.9) | copy-start | bytes 6148
  281.9 15.1 %copy-start.2 = (s32[500]{0:T(512)S(1)}, s32[500]{0:T(512)}, u32[]{:S(2)}) copy-start(s32[500]{0:T(512)} %param.13) | copy-start | bytes 6004
  281.9 15.2 %copy-start.1 = (bf16[2,16,512]{2,1,0:T(8,128)(2,1)S(1)}, bf16[2,16,512]{2,1,0:T(8,128)(2,1)}, u32[]{:S(2)}) copy-start(bf16[2,16,512]{2,1,0:T(8,128)(2,1)} %param.11) | copy-start | bytes 98308
  281.9 92.8 %all-to-all-start = ((bf16[128,2,8192]{2,1,0:T(2,128)(2,1)}), bf16[128,2,8192]{2,1,0:T(2,128)(2,1)}, u32[]{:S(2)}, u32[]{:S(2)}) async-start(bf16[128,2,8192]{2,1,0:T(2,128)(2,1)} %reshape.294), calls=%async_computation | async-start | bytes 8388608 | tf_op jit(solution)/shard_map/all_to_all | solution.py:105
  293.8 74.4 %all-gather.2.cloned.1.call-start = ((), (), s32[]{:S(2)}) async-start(), calls=%async_computation.1 | async-start | bytes 2359296 | tf_op jit(solution)/shard_map/all_gather | solution.py:96
Sparse Core Ops, SparseCore 0:
  296.3 71.8 all-gather.1
where the time goes:
time: 532 us; the launch traced here: 521 us
  local copies, waits for them, and re-layouts  285 us (54%)
  waiting for transfers between devices  105 us (20%)
  other arithmetic  61.2 us (12%)
  matrix products  39.9 us (8%)
  starting transfers between devices  15.5 us (3%)
  between operations  14.8 us (3%)
    all_gather x1, waiting for transfers between devices, shards(): table = lax.all_gather(steer, 'sect', axis=0, tiled=True)  71.1 us
    unnamed x14, local copies, waits for them, and re-layouts  61.6 us
    gather x3, local copies, waits for them, and re-layouts, shards(): jnp.take(spectra.reshape(2, stations_here, frames_here, slot_total, SUBW)...  40.7 us
    ppermute x1, waiting for transfers between devices, from_behind(): return lax.ppermute(block, axis, route)  32.8 us
    reshape x2, local copies, waits for them, and re-layouts, shards(): grid = grid.reshape(2, items, AVG, station_total, frame_total)  30 us
    reshape x1, local copies, waits for them, and re-layouts, shards(): received.reshape(2, chan_count, sect_count, items, AVG, stations_here, fr...  28.3 us
    gather x1, local copies, waits for them, and re-layouts, shards(): arranged = jnp.take(grid, inverse, axis=3)  28.1 us
    transpose x1, local copies, waits for them, and re-layouts, shards(): outgoing = jnp.transpose(picked, (0, 3, 1, 2))  23.8 us
  transfers between devices with their start and end apart: 3, of which 2 were waited for; matrix products, arithmetic and copies ran while one was open for 2% of the time, Pallas kernels for 0%

commit v1 on v0

v1 whole, which is shorter than its diff:
```python
import functools
import math

import jax
import jax.numpy as jnp
import numpy as np
from jax import lax
from jax.experimental import pallas as pl
from jax.experimental.pallas import tpu as pltpu
from jax.sharding import PartitionSpec as P

LANES = 128
HALF = 16
BLOCKS = 32
ROWS = 80
MESH = pl.DeviceIdType.MESH


def twiddles():
    k = np.arange(BLOCKS)[:, None].astype(np.float64)
    lane = np.arange(LANES)[None, :].astype(np.float64)
    angle = 2.0 * np.pi / 4096.0 * k * lane
    return np.stack([np.cos(angle), -np.sin(angle)]).astype(np.float32)


def lane_matrix(band_start):
    bins = (band_start[:, None] // 32 + jnp.arange(2, dtype=jnp.int32)[None, :]).reshape(-1)
    turn = (bins[:, None] * jnp.arange(LANES, dtype=jnp.int32)[None, :]) % LANES
    angle = (2.0 * math.pi / LANES) * turn.astype(jnp.float32)
    cosine = jnp.cos(angle) / 64.0
    sine = jnp.sin(angle) / 64.0
    upper = jnp.concatenate([cosine, sine], axis=1)
    lower = jnp.concatenate([-sine, cosine], axis=1)
    return jnp.concatenate([upper, lower], axis=0).astype(jnp.bfloat16)


def cmul_const(re, im, angle):
    c, s = math.cos(angle), math.sin(angle)
    if abs(s) < 1e-12 and c > 0:
        return re, im
    if abs(c) < 1e-12:
        return (im, -re) if s > 0 else (-im, re)
    if abs(abs(c) - abs(s)) < 1e-12 and c > 0 and s > 0:
        return (re + im) * c, (im - re) * c
    if abs(abs(c) - abs(s)) < 1e-12 and c < 0 and s > 0:
        return (im - re) * s, (im + re) * (-s)
    return re * c + im * s, im * c - re * s


def dft4(x):
    (ar, ai), (br, bi), (cr, ci), (dr, di) = x
    pr, pi = ar + cr, ai + ci
    qr, qi = ar - cr, ai - ci
    rr, ri = br + dr, bi + di
    sr, si = br - dr, bi - di
    return [
        (pr + rr, pi + ri),
        (qr + si, qi - sr),
        (pr - rr, pi - ri),
        (qr - si, qi + sr),
    ]


def dft8(x):
    even = dft4(x[0::2])
    odd = dft4(x[1::2])
    odd = [cmul_const(r, i, 2.0 * math.pi * k / 8.0) for k, (r, i) in enumerate(odd)]
    low = [(e[0] + o[0], e[1] + o[1]) for e, o in zip(even, odd)]
    high = [(e[0] - o[0], e[1] - o[1]) for e, o in zip(even, odd)]
    return low + high


def spectra_kernel(
    volt, taps, tw, mat, out, vbuf, stage, ybuf, tbuf, sbuf, load_sems, send_sems, recv_sems
):
    me_c = lax.axis_index("chan")
    me_s = lax.axis_index("sect")
    n_c = lax.axis_size("chan")
    n_s = lax.axis_size("sect")
    count = n_c * n_s
    frames = volt.shape[2] // 4096

    def load(half, f):
        return pltpu.make_async_copy(
            volt.at[:, pl.ds(half * HALF, HALF), pl.ds(f * 4096, 4096)],
            vbuf.at[half, f + 3],
            load_sems.at[half],
        )

    for half in range(2):

        @pl.loop(0, frames)
        def _(f):
            load(half, f).start()

    barrier = pltpu.get_barrier_semaphore()

    def peer(step):
        return (
            lax.rem(me_c + step // n_s, n_c),
            lax.rem(me_s + lax.rem(step, n_s), n_s),
        )

    @pl.loop(1, count)
    def _(step):
        pl.semaphore_signal(barrier, inc=1, device_id=peer(step), device_id_type=MESH)

    for half in range(2):
        for pad in range(3):
            vbuf[half, pad] = jnp.zeros(vbuf.shape[2:], vbuf.dtype)
            vbuf[half, frames + 3 + pad] = jnp.zeros(vbuf.shape[2:], vbuf.dtype)

    @pl.loop(0, 2)
    def _(half):
        pltpu.make_async_copy(
            vbuf.at[half, pl.ds(3, frames)], vbuf.at[half, pl.ds(3, frames)], load_sems.at[half]
        ).wait()

        @pl.loop(0, frames + 3)
        def _(f):
            for q0 in range(8):
                four = []
                for q1 in range(4):
                    cols = pl.ds((q0 + 8 * q1) * LANES, LANES)
                    parts = []
                    for part in range(2):
                        total = None
                        for t in range(4):
                            x = vbuf[half, f + 3 - t, part, :, cols].astype(jnp.float32)
                            term = x * taps[t : t + 1, cols]
                            total = term if total is None else total + term
                        parts.append(total)
                    four.append(tuple(parts))
                for ka, (re, im) in enumerate(dft4(four)):
                    re, im = cmul_const(re, im, 2.0 * math.pi * q0 * ka / 32.0)
                    stage[ka, q0, 0] = re
                    stage[ka, q0, 1] = im
            for ka in range(4):
                eight = [(stage[ka, q0, 0], stage[ka, q0, 1]) for q0 in range(8)]
                for kb, (re, im) in enumerate(dft8(eight)):
                    k = ka + 4 * kb
                    c = tw[0, k : k + 1, :]
                    s = tw[1, k : k + 1, :]
                    rows = pl.ds(k * HALF, HALF)
                    ybuf[rows, :LANES] = (re * c - im * s).astype(jnp.bfloat16)
                    ybuf[rows, LANES:] = (re * s + im * c).astype(jnp.bfloat16)
            own = f < frames
            for group in range(4):
                k_hi, kh = group // 2, group % 2
                res = lax.dot_general(
                    mat[...],
                    ybuf[group * LANES : (group + 1) * LANES, :],
                    (((1,), (1,)), ((), ())),
                    preferred_element_type=jnp.float32,
                )
                for part in range(2):
                    base = jnp.where(
                        own,
                        k_hi * ROWS + kh * 32 + part * 16 + f,
                        k_hi * ROWS + 64 + kh * 8 + part * 4 + f - frames,
                    )
                    tbuf[pl.ds(base, 64, stride=2 * ROWS), :] = res[part * 64 : (part + 1) * 64]

        @pl.when(half == 0)
        def _():
            pl.semaphore_wait(barrier, count - 1)

        slot = me_s * n_c + me_c

        @pl.loop(0, count)
        def _(step):
            c, s = peer(step)
            dest = c * n_s + s
            block = tbuf[pl.ds(pl.multiple_of(dest * ROWS, 8), ROWS), :]
            sbuf[half, dest] = block.astype(jnp.bfloat16)

            @pl.when(step > 0)
            def _():
                pltpu.make_async_remote_copy(
                    src_ref=sbuf.at[half, dest],
                    dst_ref=out.at[half, slot],
                    send_sem=send_sems.at[half],
                    recv_sem=recv_sems.at[half],
                    device_id=(c, s),
                    device_id_type=MESH,
                ).start()

            @pl.when(step == 0)
            def _():
                pltpu.make_async_copy(
                    sbuf.at[half, dest], out.at[half, slot], recv_sems.at[half]
                ).start()

    for half in range(2):
        pltpu.make_async_copy(out.at[half], out.at[half], recv_sems.at[half]).wait()
        pltpu.make_async_copy(
            sbuf.at[half, pl.ds(0, count - 1)],
            sbuf.at[half, pl.ds(0, count - 1)],
            send_sems.at[half],
        ).wait()


def channelize(voltages, fir_taps, band_start):
    count = lax.axis_size("chan") * lax.axis_size("sect")
    frames = voltages.shape[2] // 4096
    hbm = pl.BlockSpec(memory_space=pl.ANY)
    vmem = pl.BlockSpec(memory_space=pltpu.VMEM)
    return pl.pallas_call(
        spectra_kernel,
        out_shape=jax.ShapeDtypeStruct((2, count, ROWS, LANES), jnp.bfloat16),
        in_specs=[hbm, vmem, vmem, vmem],
        out_specs=hbm,
        scratch_shapes=[
            pltpu.VMEM((2, frames + 6, 2, HALF, 4096), jnp.bfloat16),
            pltpu.VMEM((4, 8, 2, HALF, LANES), jnp.float32),
            pltpu.VMEM((BLOCKS * HALF, 2 * LANES), jnp.bfloat16),
            pltpu.VMEM((count * ROWS, LANES), jnp.float32),
            pltpu.VMEM((2, count, ROWS, LANES), jnp.bfloat16),
            pltpu.SemaphoreType.DMA((2,)),
            pltpu.SemaphoreType.DMA((2,)),
            pltpu.SemaphoreType.DMA((2,)),
        ],
        compiler_params=pltpu.CompilerParams(
            collective_id=0, has_side_effects=True, vmem_limit_bytes=56 * 1024 * 1024
        ),
        name="spectra",
    )(voltages, fir_taps, jnp.asarray(twiddles()), lane_matrix(band_start))


def swap_blocks(tiles):
    lane = lax.broadcasted_iota(jnp.int32, tiles[0].shape, 1)
    tiles = list(tiles)
    for bit in (4, 2, 1):
        upper = (lane // (bit * 16)) % 2 == 1
        for j in range(8):
            if j & bit == 0:
                a, b = tiles[j], tiles[j + bit]
                tiles[j] = jnp.where(upper, pltpu.roll(b, bit * 16, 1), a)
                tiles[j + bit] = jnp.where(upper, b, pltpu.roll(a, LANES - bit * 16, 1))
    return tiles


NT = (((1,), (1,)), ((), ()))


def dot_nt(a, b):
    return lax.dot_general(a, b, NT, preferred_element_type=jnp.float32)


def product_kernel(
    scale, recv, order, calib, steer, pick, vis, beams, xt, ct, gains, weights, zbuf, wbuf
):
    n_s = 8
    n_c = 16

    @pl.when(pl.program_id(0) == 0)
    def _():
        gains[...] = jnp.dot(calib[...], order[...], preferred_element_type=jnp.float32)
        picked = jnp.dot(pick[...], steer[...], preferred_element_type=jnp.float32)
        picked = picked.astype(jnp.bfloat16)
        for part in range(2):
            weights[part * 512 : (part + 1) * 512, :] = jnp.dot(
                picked[:, part * 512 : (part + 1) * 512],
                order[...],
                preferred_element_type=jnp.float32,
            ).astype(jnp.bfloat16)

        @pl.loop(0, n_s)
        def _(s):
            before = jnp.maximum(s - 1, 0)
            row = lax.broadcasted_iota(jnp.int32, (8, LANES), 0)
            keep = (row < 3) & (s > 0)
            for half in range(2):
                for c_hi in range(2):
                    group = half * 2 + c_hi
                    cols = slice(group * LANES, (group + 1) * LANES)
                    for kh in range(2):
                        done = []
                        for part in range(2):
                            tiles = []
                            for c_lo in range(8):
                                c = c_hi * 8 + c_lo
                                rows = pl.ds((kh * 2 + part) * 16, 16)
                                own = recv[half, s * n_c + c, rows, :].astype(jnp.float32)
                                extra = recv[half, before * n_c + c, 64:80, :]
                                extra = extra.astype(jnp.float32)[kh * 8 : kh * 8 + 8]
                                if part == 1:
                                    extra = pltpu.roll(extra, 4, 0)
                                first = own[:8] + jnp.where(keep, extra, 0.0)
                                tiles.append(jnp.concatenate([first, own[8:]], axis=0))
                            done.append(swap_blocks(tiles))
                        for k8 in range(8):
                            ch = kh * 8 + k8
                            real = done[0][k8].astype(jnp.bfloat16)
                            imag = done[1][k8].astype(jnp.bfloat16)
                            low = pl.ds(pl.multiple_of(s * 16, 16), 16)
                            high = pl.ds(pl.multiple_of(128 + s * 16, 16), 16)
                            xt[ch, low, cols] = real
                            xt[ch, high, cols] = imag
                            real = real.astype(jnp.float32)
                            imag = imag.astype(jnp.float32)
                            g_re = gains[ch : ch + 1, cols]
                            g_im = gains[16 + ch : 17 + ch, cols]
                            ct[ch, low, cols] = (g_re * real - g_im * imag).astype(jnp.bfloat16)
                            ct[ch, high, cols] = (g_re * imag + g_im * real).astype(jnp.bfloat16)

    g = pl.program_id(0)
    for a in range(4):
        z = dot_nt(order[...], xt[g * 4 + a]).astype(jnp.bfloat16)
        zbuf[:, a * 256 : (a + 1) * 256] = z
        wbuf[:, a * 256 : a * 256 + 128] = z[:, 128:]
        wbuf[:, a * 256 + 128 : (a + 1) * 256] = -z[:, :128]
    vis[0, 0] = dot_nt(zbuf[...], zbuf[...]) * scale
    vis[1, 0] = dot_nt(wbuf[...], zbuf[...]) * scale
    n_b = beams.shape[2]
    for a in range(4):
        uv = dot_nt(weights[...], ct[g * 4 + a])
        beams[0, a] = (uv[:n_b, :128] - uv[512 : 512 + n_b, 128:]).astype(jnp.bfloat16)
        beams[1, a] = (uv[:n_b, 128:] + uv[512 : 512 + n_b, :128]).astype(jnp.bfloat16)


def products(received, station_map, calib, table, beam_index):
    rank = jnp.arange(512, dtype=jnp.int32)
    row_of = (rank // 16 % 16) * 32 + (rank // 256) * 16 + rank % 16
    place = station_map.reshape(16, 2, 16).transpose(1, 0, 2).reshape(-1)
    del row_of
    order = (place[None, :] == rank[:, None]).astype(jnp.bfloat16)
    padded = jnp.pad(beam_index, (0, 12), constant_values=-1)
    pick = (padded[:, None] == jnp.arange(1024, dtype=jnp.int32)[None, :]).astype(jnp.bfloat16)
    whole = lambda *dims: pl.BlockSpec(dims, lambda g: (0,) * len(dims))
    return pl.pallas_call(
        functools.partial(product_kernel, 1.0 / 512.0),
        grid=(4,),
        out_shape=(
            jax.ShapeDtypeStruct((2, 4, 512, 512), jnp.float32),
            jax.ShapeDtypeStruct((2, 16, 500, 128), jnp.bfloat16),
        ),
        in_specs=[
            whole(2, 128, ROWS, LANES),
            whole(512, 512),
            whole(32, 512),
            whole(1024, 1024),
            whole(512, 1024),
        ],
        out_specs=(
            pl.BlockSpec((2, 1, 512, 512), lambda g: (0, g, 0, 0)),
            pl.BlockSpec((2, 4, 500, 128), lambda g: (0, g, 0, 0)),
        ),
        scratch_shapes=[
            pltpu.VMEM((16, 256, 512), jnp.bfloat16),
            pltpu.VMEM((16, 256, 512), jnp.bfloat16),
            pltpu.VMEM((32, 512), jnp.float32),
            pltpu.VMEM((1024, 512), jnp.bfloat16),
            pltpu.VMEM((512, 1024), jnp.bfloat16),
            pltpu.VMEM((512, 1024), jnp.bfloat16),
        ],
        compiler_params=pltpu.CompilerParams(vmem_limit_bytes=56 * 1024 * 1024),
        name="products",
    )(received, order, calib.reshape(32, 512), table.reshape(1024, 1024), pick)


def shards(voltages, fir_taps, station_map, band_start, calib, steer, beam_index):
    table = lax.all_gather(steer, "sect", axis=0, tiled=True)
    received = channelize(voltages, fir_taps, band_start)
    return products(received, station_map, calib, table, beam_index)


def solution(mesh):
    return jax.shard_map(
        shards,
        mesh=mesh,
        in_specs=(
            P(None, "chan", "sect"),
            P(),
            P(),
            P(),
            P(None, ("chan", "sect"), None),
            P("sect", None, None),
            P(),
        ),
        out_specs=(P(None, ("chan", "sect"), None, None), P(None, ("chan", "sect"), None, None)),
        check_vma=False,
    )
```

time: 532 us -> 165 us (0.31)
  the two profiles are of different devices: /device:TPU:4 before, /device:TPU:1 now
where the time goes in v1:
time: 165 us
  Pallas kernels  136 us (82%)
  between operations  14.1 us (9%)
  local copies, waits for them, and re-layouts  9.8 us (6%)
  other arithmetic  3.77 us (2%)
    pallas_call x1, Pallas kernels, channelize(): pl.pallas_call(spectra_kernel, out_shape=jax.ShapeDtypeStruct((2, count,...  103 us
    pallas_call x1, Pallas kernels, products(): pl.pallas_call(functools.partial(product_kernel, 1.0 / 512.0), grid=(4,),...  33.7 us
    pallas_call x1, local copies, waits for them, and re-layouts, products(): pl.pallas_call(functools.partial(product_kernel, 1.0 / 512.0), grid=(4,),...  4.67 us
    unnamed x1, local copies, waits for them, and re-layouts  3.48 us
  transfers between devices with their start and end apart: 1, of which 0 were waited for; matrix products, arithmetic and copies ran while one was open for 3% of the time, Pallas kernels for 62%

profile of v1, /device:TPU:1, one launch (start us, length us, event | category | flops | bytes accessed | tf_op | source)
XLA Modules:
  0.0 164.8 jit_solution(13217644346254511129)
XLA Ops:
  7.2 0.0 all-gather.2.cloned.1.call-start
  7.2 0.7 all-gather.2.cloned.1.call-update
  7.9 0.7 and_select_fusion
  8.6 0.1 iota_add_fusion
  8.6 0.1 add.33
  8.7 0.8 reshape.48
  9.5 0.1 eq.30
  9.6 0.7 pad.4
  10.3 0.2 fusion.8
  10.5 0.6 maximum_maximum_fusion.mat
  11.2 102.7 %spectra.1.recv = bf16[2,128,80,128]{3,2,1,0:T(8,128)(2,1)} custom-call(bf16[2,32,65536]{2,1,0:T(8,128)(2,1)} %volt.1, f32[4,4096]{1,0:T(4,128)} %taps.1, f32[2,32,128]{2,1,0:T(8,128)} %constant.39.clone.tw, bf16[128,256]{1,0:T(8,128)(2,1)} %maximum_maximum_fusion.mat), custom_call_target="tpu_custom_call" | custom-call | tf_op jit(solution)/shard_map/spectra/pallas_call | solution.py:208
  113.9 1.0 fusion.1.order
  114.8 1.2 fusion.pick
  116.0 0.0 all-gather.2.cloned.1.call-done
  116.0 3.5 %copy.16 = bf16[128,8,2,512]{3,1,2,0:T(8,128)(2,1)} copy(bf16[128,8,2,512]{3,2,1,0:T(2,128)(2,1)} %bitcast.5) | data formatting | bytes 4194304
  119.5 33.7 %products.1 = (f32[2,4,512,512]{3,2,1,0:T(8,128)}, bf16[2,16,500,128]{3,2,1,0:T(8,128)(2,1)}) custom-call(bf16[2,128,80,128]{3,2,1,0:T(8,128)(2,1)} %spectra.1.recv, bf16[512,512]{1,0:T(8,128)(2,1)} %fusion.1.order, bf16[32,512]{1,0:T(8,128)(2,1)} %bitcast.7, bf16[1024,1024]{1,0:T(8,128)(2,1)} %bitcast.4, bf16[512,1024]{1,0:T(8,128)(2,1)} %fusion.pick), custom_call_target="tpu_custom_call" | custom-call | tf_op jit(solution)/shard_map/products/pallas_call | solution.py:331
  153.3 4.7 %copy.15 = bf16[2,16,500,128]{3,1,2,0:T(8,128)(2,1)} copy(bf16[2,16,500,128]{3,2,1,0:T(8,128)(2,1)} %get-tuple-element.9) | data formatting | bytes 8192000 | tf_op jit(solution)/shard_map/products/pallas_call | solution.py:331
  (1 shorter events, 0.0 us)
Async XLA Ops:
  7.2 108.9 %all-gather.2.cloned.1.call-start = ((), (), s32[]{:S(2)}) async-start(), calls=%async_computation | async-start | bytes 2359296 | tf_op jit(solution)/shard_map/all_gather | solution.py:363
Sparse Core Ops, SparseCore 0:
  9.6 99.1 all-gather.1

commit v2 on v1

v2 whole, which is shorter than its diff:
```python
import functools
import math

import jax
import jax.numpy as jnp
import numpy as np
from jax import lax
from jax.experimental import pallas as pl
from jax.experimental.pallas import tpu as pltpu
from jax.sharding import PartitionSpec as P

LANES = 128
HALF = 16
BLOCKS = 32
ROWS = 80
MESH = pl.DeviceIdType.MESH


def twiddles():
    k = np.arange(BLOCKS)[:, None].astype(np.float64)
    lane = np.arange(LANES)[None, :].astype(np.float64)
    angle = 2.0 * np.pi / 4096.0 * k * lane
    return np.stack([np.cos(angle), -np.sin(angle)]).astype(np.float32)


def lane_matrix(band_start):
    bins = (band_start[:, None] // 32 + jnp.arange(2, dtype=jnp.int32)[None, :]).reshape(-1)
    turn = (bins[:, None] * jnp.arange(LANES, dtype=jnp.int32)[None, :]) % LANES
    angle = (2.0 * math.pi / LANES) * turn.astype(jnp.float32)
    cosine = jnp.cos(angle) / 64.0
    sine = jnp.sin(angle) / 64.0
    upper = jnp.concatenate([cosine, sine], axis=1)
    lower = jnp.concatenate([-sine, cosine], axis=1)
    return jnp.concatenate([upper, lower], axis=0).astype(jnp.bfloat16)


def cmul_const(re, im, angle):
    c, s = math.cos(angle), math.sin(angle)
    if abs(s) < 1e-12 and c > 0:
        return re, im
    if abs(c) < 1e-12:
        return (im, -re) if s > 0 else (-im, re)
    if abs(abs(c) - abs(s)) < 1e-12 and c > 0 and s > 0:
        return (re + im) * c, (im - re) * c
    if abs(abs(c) - abs(s)) < 1e-12 and c < 0 and s > 0:
        return (im - re) * s, (im + re) * (-s)
    return re * c + im * s, im * c - re * s


def dft4(x):
    (ar, ai), (br, bi), (cr, ci), (dr, di) = x
    pr, pi = ar + cr, ai + ci
    qr, qi = ar - cr, ai - ci
    rr, ri = br + dr, bi + di
    sr, si = br - dr, bi - di
    return [
        (pr + rr, pi + ri),
        (qr + si, qi - sr),
        (pr - rr, pi - ri),
        (qr - si, qi + sr),
    ]


def dft8(x):
    even = dft4(x[0::2])
    odd = dft4(x[1::2])
    odd = [cmul_const(r, i, 2.0 * math.pi * k / 8.0) for k, (r, i) in enumerate(odd)]
    low = [(e[0] + o[0], e[1] + o[1]) for e, o in zip(even, odd)]
    high = [(e[0] - o[0], e[1] - o[1]) for e, o in zip(even, odd)]
    return low + high


NT = (((1,), (1,)), ((), ()))
TN = (((0,), (0,)), ((), ()))


def dot(a, b, dims=(((1,), (0,)), ((), ()))):
    return lax.dot_general(a, b, dims, preferred_element_type=jnp.float32)


def iota(shape, dim):
    return lax.broadcasted_iota(jnp.int32, shape, dim)


def one_hot(found):
    return jnp.where(found, 1.0, 0.0).astype(jnp.bfloat16)


def spectra_kernel(
    volt, steer, emat, taps, tw, mat, smap, bidx, calib,
    xt_out, ct_out, w_out, order_out,
    vbuf, stage, ybuf, tbuf, sbuf, rbuf, xin, res, ebuf, xt, ct, order, gains, table, wpart,
    wall, weights, load_sems, send_sems, recv_sems, steer_sems, out_sems,
):
    me_c = lax.axis_index("chan")
    me_s = lax.axis_index("sect")
    n_c = lax.axis_size("chan")
    n_s = lax.axis_size("sect")
    count = n_c * n_s
    frames = volt.shape[2] // 4096
    core = lax.rem(me_c, 2)
    chip = me_c // 2
    my_x = lax.rem(chip, 2) * 2 + me_s // 4
    my_y = lax.rem(me_s, 4)
    my_z = chip // 2

    def load(half, f):
        return pltpu.make_async_copy(
            volt.at[:, pl.ds(half * HALF, HALF), pl.ds(f * 4096, 4096)],
            vbuf.at[half, f + 3],
            load_sems.at[half],
        )

    for half in range(2):

        @pl.loop(0, frames)
        def _(f):
            load(half, f).start()

    fetch_e = pltpu.make_async_copy(emat, ebuf, steer_sems.at[4])
    fetch_e.start()

    barrier = pltpu.get_barrier_semaphore()

    @pl.loop(1, count)
    def _(step):
        c = lax.rem(me_c + step // n_s, n_c)
        s = lax.rem(me_s + lax.rem(step, n_s), n_s)
        pl.semaphore_signal(barrier, inc=1, device_id=(c, s), device_id_type=MESH)

    for half in range(2):
        for pad in range(3):
            vbuf[half, pad] = jnp.zeros(vbuf.shape[2:], vbuf.dtype)
            vbuf[half, frames + 3 + pad] = jnp.zeros(vbuf.shape[2:], vbuf.dtype)

    pl.semaphore_wait(barrier, count - 1)

    share = steer.at[:, pl.ds(pl.multiple_of(chip * LANES, LANES), LANES)]

    @pl.loop(1, n_s)
    def _(step):
        pltpu.make_async_remote_copy(
            src_ref=share,
            dst_ref=table.at[me_s],
            send_sem=steer_sems.at[0],
            recv_sem=steer_sems.at[1],
            device_id=(me_c, lax.rem(me_s + step, n_s)),
            device_id_type=MESH,
        ).start()

    pltpu.make_async_copy(share, table.at[me_s], steer_sems.at[1]).start()

    def pick_and_share():
        pltpu.make_async_copy(table, table, steer_sems.at[1]).wait()
        total = None
        for s in range(8):
            found = bidx[...] == iota((LANES, 512), 0) + s * LANES
            term = dot(one_hot(found), table[s], TN)
            total = term if total is None else total + term
        wpart[...] = total.astype(jnp.bfloat16)

        @pl.loop(1, 8)
        def _(step):
            pltpu.make_async_remote_copy(
                src_ref=wpart,
                dst_ref=wall.at[chip],
                send_sem=steer_sems.at[2],
                recv_sem=steer_sems.at[3],
                device_id=(lax.rem(chip + step, 8) * 2 + core, me_s),
                device_id_type=MESH,
            ).start()

        pltpu.make_async_copy(wpart, wall.at[chip], steer_sems.at[3]).start()

    def one_frame(half, f):
        for q0 in range(8):
            four = []
            for q1 in range(4):
                cols = pl.ds((q0 + 8 * q1) * LANES, LANES)
                parts = []
                for part in range(2):
                    total = None
                    for t in range(4):
                        x = vbuf[half, f + 3 - t, part, :, cols].astype(jnp.float32)
                        term = x * taps[t : t + 1, cols]
                        total = term if total is None else total + term
                    parts.append(total)
                four.append(tuple(parts))
            for ka, (re, im) in enumerate(dft4(four)):
                re, im = cmul_const(re, im, 2.0 * math.pi * q0 * ka / 32.0)
                stage[ka, q0, 0] = re
                stage[ka, q0, 1] = im
        for ka in range(4):
            eight = [(stage[ka, q0, 0], stage[ka, q0, 1]) for q0 in range(8)]
            for kb, (re, im) in enumerate(dft8(eight)):
                k = ka + 4 * kb
                c = tw[0, k : k + 1, :]
                s = tw[1, k : k + 1, :]
                rows = pl.ds(k * HALF, HALF)
                ybuf[rows, :LANES] = (re * c - im * s).astype(jnp.bfloat16)
                ybuf[rows, LANES:] = (re * s + im * c).astype(jnp.bfloat16)
        own = f < frames
        for group in range(4):
            k_hi, kh = group // 2, group % 2
            out = dot(mat[...], ybuf[group * LANES : (group + 1) * LANES, :], NT)
            for part in range(2):
                base = k_hi * ROWS + jnp.where(
                    own,
                    f // 8 * 32 + kh * 16 + part * 8 + lax.rem(f, 8),
                    64 + kh * 8 + part * 4 + f - frames,
                )
                tbuf[pl.ds(base, 64, stride=2 * ROWS), :] = out[part * 64 : (part + 1) * 64]

    slot = me_s * n_c + me_c

    def send_out(half, late):
        rows = pl.ds(32, 48) if late else pl.ds(0, 32)

        @pl.loop(0, count // 2)
        def _(step):
            k0 = lax.rem(step, 4)
            k1 = lax.rem(step // 4, 4)
            k2 = step // 16
            x = lax.rem(my_x + k0, 4)
            y = lax.rem(my_y + k0 + k1, 4)
            z = lax.rem(my_z + k0 + k1 + k2, 4)
            for flip in range(2):
                c = (z * 2 + x // 2) * 2 + lax.rem(core + flip, 2)
                s = lax.rem(x, 2) * 4 + y
                dest = c * n_s + s
                first = pl.multiple_of(dest * ROWS + (32 if late else 0), 8)
                block = tbuf[pl.ds(first, 48 if late else 32), :]
                sbuf[half, dest, rows] = block.astype(jnp.bfloat16)

                def go():
                    pltpu.make_async_remote_copy(
                        src_ref=sbuf.at[half, dest, rows],
                        dst_ref=rbuf.at[half, slot, rows],
                        send_sem=send_sems.at[half, late],
                        recv_sem=recv_sems.at[half, late],
                        device_id=(c, s),
                        device_id_type=MESH,
                    ).start()

                if flip:
                    go()
                else:
                    pl.when(step > 0)(go)

                    @pl.when(step == 0)
                    def _():
                        pltpu.make_async_copy(
                            sbuf.at[half, dest, rows],
                            rbuf.at[half, slot, rows],
                            recv_sems.at[half, late],
                        ).start()

    @pl.loop(0, 2)
    def _(half):
        pltpu.make_async_copy(
            vbuf.at[half, pl.ds(3, frames)], vbuf.at[half, pl.ds(3, frames)], load_sems.at[half]
        ).wait()

        @pl.loop(0, 8)
        def _(f):
            one_frame(half, f)

            @pl.when((half == 0) & (f == 4))
            def _():
                pick_and_share()

        send_out(half, 0)

        @pl.loop(8, frames + 3)
        def _(f):
            one_frame(half, f)

        send_out(half, 1)

    rank = iota((512, 512), 1)
    natural = lax.rem(rank // 16, 16) * 32 + rank // 256 * 16 + lax.rem(rank, 16)
    move = one_hot(iota((512, 512), 0) == natural)
    order[...] = dot(one_hot(smap[...] == iota((512, 512), 0)), move).astype(jnp.bfloat16)
    gains[...] = dot(calib[...], order[...])
    pltpu.make_async_copy(wall, wall, steer_sems.at[3]).wait()
    for part in range(2):
        picked = jnp.concatenate([wall[part * 4 + j] for j in range(4)], axis=1)
        weights[part * 512 : (part + 1) * 512, :] = dot(picked, order[...]).astype(jnp.bfloat16)
    put = [
        pltpu.make_async_copy(weights, w_out, out_sems.at[0]),
        pltpu.make_async_copy(order, order_out, out_sems.at[1]),
    ]
    for copy in put:
        copy.start()
    fetch_e.wait()

    row = iota((8, LANES), 0)
    for half in range(2):
        for late in range(2):
            rows = pl.ds(32, 48) if late else pl.ds(0, 32)
            pltpu.make_async_copy(
                rbuf.at[half, :, rows], rbuf.at[half, :, rows], recv_sems.at[half, late]
            ).wait()
        for c_hi in range(2):
            cols = slice(half * 256 + c_hi * LANES, half * 256 + (c_hi + 1) * LANES)
            for kh in range(2):

                @pl.loop(0, n_s)
                def _(s):
                    before = jnp.maximum(s - 1, 0)
                    keep = (row < 3) & (s > 0)
                    low = pl.ds(pl.multiple_of(s * 32, 32), 16)
                    high = pl.ds(pl.multiple_of(s * 32 + 16, 16), 16)
                    for c_lo in range(8):
                        c = c_hi * 8 + c_lo
                        at = s * n_c + c
                        lanes = slice(c_lo * LANES, (c_lo + 1) * LANES)
                        early = rbuf[half, at, kh * 16 : kh * 16 + 16].astype(jnp.float32)
                        extra = rbuf[half, before * n_c + c, 64:80].astype(jnp.float32)
                        extra = extra[kh * 8 : kh * 8 + 8]
                        extra = jnp.concatenate(
                            [
                                jnp.where(keep, extra, 0.0),
                                jnp.where(keep, pltpu.roll(extra, 4, 0), 0.0),
                            ],
                            axis=0,
                        )
                        xin[low, lanes] = (early + extra).astype(jnp.bfloat16)
                        xin[high, lanes] = rbuf[half, at, 32 + kh * 16 : 48 + kh * 16]

                res[...] = dot(xin[...], ebuf[...])

                @pl.loop(0, n_s)
                def _(s):
                    low = pl.ds(pl.multiple_of(s * 16, 16), 16)
                    high = pl.ds(pl.multiple_of(128 + s * 16, 16), 16)
                    for k8 in range(8):
                        ch = kh * 8 + k8
                        lanes = slice(k8 * LANES, (k8 + 1) * LANES)
                        quarter = [
                            res[pl.ds(pl.multiple_of(s * 32 + 8 * j, 8), 8), lanes]
                            for j in range(4)
                        ]
                        real = jnp.concatenate([quarter[0], quarter[2]], axis=0)
                        imag = jnp.concatenate([quarter[1], quarter[3]], axis=0)
                        xt[ch, low, cols] = real.astype(jnp.bfloat16)
                        xt[ch, high, cols] = imag.astype(jnp.bfloat16)
                        g_re = gains[ch : ch + 1, cols]
                        g_im = gains[16 + ch : 17 + ch, cols]
                        ct[ch, low, cols] = (g_re * real - g_im * imag).astype(jnp.bfloat16)
                        ct[ch, high, cols] = (g_re * imag + g_im * real).astype(jnp.bfloat16)

        cols = pl.ds(half * 256, 256)
        for k, (src, dst) in enumerate(((xt, xt_out), (ct, ct_out))):
            put.append(
                pltpu.make_async_copy(
                    src.at[:, :, cols], dst.at[:, :, cols], out_sems.at[2 + half * 2 + k]
                )
            )
            put[-1].start()

    for copy in put:
        copy.wait()
    for half in range(2):
        for late in range(2):
            rows = pl.ds(32, 48) if late else pl.ds(0, 32)
            sent = sbuf.at[half, pl.ds(0, count - 1), rows]
            pltpu.make_async_copy(sent, sent, send_sems.at[half, late]).wait()
    sent = table.at[pl.ds(0, 7)]
    pltpu.make_async_copy(sent, sent, steer_sems.at[0]).wait()
    sent = wall.at[pl.ds(0, 7)]
    pltpu.make_async_copy(sent, sent, steer_sems.at[2]).wait()


def block_swap():
    line = np.arange(1024)
    source = (line // 16 % 8) * LANES + (line // LANES) * 16 + line % 16
    out = np.zeros((1024, 1024), np.float32)
    out[source, line] = 1.0
    return out.astype(jnp.bfloat16)


def channelize(voltages, fir_taps, band_start, steer, station_map, beam_index, calib):
    count = lax.axis_size("chan") * lax.axis_size("sect")
    frames = voltages.shape[2] // 4096
    hbm = pl.BlockSpec(memory_space=pl.ANY)
    vmem = pl.BlockSpec(memory_space=pltpu.VMEM)
    half16 = jnp.bfloat16
    return pl.pallas_call(
        spectra_kernel,
        out_shape=(
            jax.ShapeDtypeStruct((16, 256, 512), half16),
            jax.ShapeDtypeStruct((16, 256, 512), half16),
            jax.ShapeDtypeStruct((1024, 512), half16),
            jax.ShapeDtypeStruct((512, 512), half16),
        ),
        in_specs=[hbm] * 3 + [vmem] * 6,
        out_specs=(hbm,) * 4,
        scratch_shapes=[
            pltpu.VMEM((2, frames + 6, 2, HALF, 4096), half16),
            pltpu.VMEM((4, 8, 2, HALF, LANES), jnp.float32),
            pltpu.VMEM((BLOCKS * HALF, 2 * LANES), half16),
            pltpu.VMEM((count * ROWS, LANES), jnp.float32),
            pltpu.VMEM((2, count, ROWS, LANES), half16),
            pltpu.VMEM((2, count, ROWS, LANES), half16),
            pltpu.VMEM((256, 1024), half16),
            pltpu.VMEM((256, 1024), jnp.float32),
            pltpu.VMEM((1024, 1024), half16),
            pltpu.VMEM((16, 256, 512), half16),
            pltpu.VMEM((16, 256, 512), half16),
            pltpu.VMEM((512, 512), half16),
            pltpu.VMEM((32, 512), jnp.float32),
            pltpu.VMEM((8, LANES, LANES), half16),
            pltpu.VMEM((512, LANES), half16),
            pltpu.VMEM((8, 512, LANES), half16),
            pltpu.VMEM((1024, 512), half16),
            pltpu.SemaphoreType.DMA((2,)),
            pltpu.SemaphoreType.DMA((2, 2)),
            pltpu.SemaphoreType.DMA((2, 2)),
            pltpu.SemaphoreType.DMA((5,)),
            pltpu.SemaphoreType.DMA((6,)),
        ],
        compiler_params=pltpu.CompilerParams(
            collective_id=0, has_side_effects=True, vmem_limit_bytes=60 * 1024 * 1024
        ),
        name="spectra",
    )(
        voltages,
        steer.reshape(LANES, 1024),
        jnp.asarray(block_swap()),
        fir_taps,
        jnp.asarray(twiddles()),
        lane_matrix(band_start),
        station_map.reshape(1, 512),
        jnp.pad(beam_index, (0, 12), constant_values=-1).reshape(1, 512),
        calib.reshape(32, 512),
    )


def product_kernel(scale, xt, ct, weights, order, vis, beams, zbuf, wbuf, bbuf, obuf, sem):
    step = pl.program_id(0)
    n_b = beams.shape[1]
    tiles = bbuf.shape[0]

    def put(part):
        return pltpu.make_async_copy(
            obuf.at[part, pl.ds(0, n_b)], beams.at[part], sem.at[part]
        )

    @pl.when(step < 4)
    def _():
        for a in range(4):
            uv = dot(weights[...], ct[a], NT)
            real = uv[:512, :128] - uv[512:, 128:]
            imag = uv[:512, 128:] + uv[512:, :128]
            both = jnp.concatenate([real, imag], axis=1).astype(jnp.bfloat16)
            rows = pl.ds(pl.multiple_of(step * 64 + a * 16, 16), 16)
            bbuf[:, rows, :] = both.reshape(tiles, 16, 256)

    @pl.when(step == 3)
    def _():
        line = iota((256, 256), 0)
        source = lax.rem(line, 16) * 16 + line // 16
        move = one_hot(iota((256, 256), 1) == source)

        @pl.loop(0, tiles)
        def _(tile):
            out = dot(move, bbuf[tile]).astype(jnp.bfloat16)
            for part in range(2):
                piece = out[:, part * 128 : (part + 1) * 128].reshape(16, 16, 128)
                obuf[part, pl.ds(tile * 16, 16)] = piece

        for part in range(2):
            put(part).start()

    @pl.when(step >= 4)
    def _():
        for a in range(4):
            z = dot(order[...], xt[a], NT).astype(jnp.bfloat16)
            zbuf[:, a * 256 : (a + 1) * 256] = z
            wbuf[:, a * 256 : a * 256 + 128] = z[:, 128:]
            wbuf[:, a * 256 + 128 : (a + 1) * 256] = -z[:, :128]
        vis[0, 0] = dot(zbuf[...], zbuf[...], NT) * scale
        vis[1, 0] = dot(wbuf[...], zbuf[...], NT) * scale

    @pl.when(step == 7)
    def _():
        for part in range(2):
            put(part).wait()


def products(xt, ct, weights, order):
    half16 = jnp.bfloat16
    vis, beams = pl.pallas_call(
        functools.partial(product_kernel, 1.0 / 512.0),
        grid=(8,),
        out_shape=(
            jax.ShapeDtypeStruct((2, 4, 512, 512), jnp.float32),
            jax.ShapeDtypeStruct((2, 500, 16, 128), half16),
        ),
        in_specs=[
            pl.BlockSpec((4, 256, 512), lambda i: (jnp.maximum(i - 4, 0), 0, 0)),
            pl.BlockSpec((4, 256, 512), lambda i: (jnp.minimum(i, 3), 0, 0)),
            pl.BlockSpec((1024, 512), lambda i: (0, 0)),
            pl.BlockSpec((512, 512), lambda i: (0, 0)),
        ],
        out_specs=(
            pl.BlockSpec((2, 1, 512, 512), lambda i: (0, jnp.maximum(i - 4, 0), 0, 0)),
            pl.BlockSpec(memory_space=pl.ANY),
        ),
        scratch_shapes=[
            pltpu.VMEM((512, 1024), half16),
            pltpu.VMEM((512, 1024), half16),
            pltpu.VMEM((32, 256, 256), half16),
            pltpu.VMEM((2, 512, 16, 128), half16),
            pltpu.SemaphoreType.DMA((2,)),
        ],
        compiler_params=pltpu.CompilerParams(vmem_limit_bytes=56 * 1024 * 1024),
        name="products",
    )(xt, ct, weights, order)
    return vis, jnp.transpose(beams, (0, 2, 1, 3))


def shards(voltages, fir_taps, station_map, band_start, calib, steer, beam_index):
    parts = channelize(
        voltages, fir_taps, band_start, steer, station_map, beam_index, calib
    )
    return products(*parts)


def solution(mesh):
    return jax.shard_map(
        shards,
        mesh=mesh,
        in_specs=(
            P(None, "chan", "sect"),
            P(),
            P(),
            P(),
            P(None, ("chan", "sect"), None),
            P("sect", None, None),
            P(),
        ),
        out_specs=(P(None, ("chan", "sect"), None, None), P(None, ("chan", "sect"), None, None)),
        check_vma=False,
    )
```

time: 165 us -> 126 us (0.76)
  Pallas kernels: 136 us -> 121 us
  between operations: 14.1 us -> 0.65 us
  local copies, waits for them, and re-layouts: 9.8 us -> 3.05 us
  other arithmetic: 3.77 us -> 1.6 us
    pallas_call x2, Pallas kernels: 136 us -> 121 us  [the longest x1 98 us: channelize(): pl.pallas_call(spectra_kernel, out_shape=(jax.ShapeDtypeStruct((16, 256,...]
    pallas_call x1 -> x0, local copies, waits for them, and re-layouts: 4.67 us -> none  [products(): pl.pallas_call(functools.partial(product_kernel, 1.0 / 512.0), grid=(4,),...]
    convert_element_type x2 -> x0, other arithmetic: 2.17 us -> none  [the longest x1 1.21 us: products(): (padded[:, None] == jnp.arange(1024, dtype=jnp.int32)[None, :]).astype(jn...]
    unnamed x1, local copies, waits for them, and re-layouts: 3.48 us -> 1.69 us
  transfers between devices with their start and end apart: 1 -> 0, of which waited for: 0 -> 0; matrix products, arithmetic and copies ran while one was open for 3% -> 0% of each run, Pallas kernels for 62% -> 0%
where the time goes in v2:
time: 126 us
  Pallas kernels  121 us (96%)
  local copies, waits for them, and re-layouts  3.05 us (2%)
  other arithmetic  1.6 us (1%)
    pallas_call x1, Pallas kernels, channelize(): pl.pallas_call(spectra_kernel, out_shape=(jax.ShapeDtypeStruct((16, 256,...  98 us
    pallas_call x1, Pallas kernels, products(): pl.pallas_call(functools.partial(product_kernel, 1.0 / 512.0), grid=(8,),...  22.7 us

profile of v2, /device:TPU:1, one launch (start us, length us, event | category | flops | bytes accessed | tf_op | source)
XLA Modules:
  0.0 126.0 jit_solution(15491799906744635373)
XLA Ops:
  0.6 0.7 and_select_fusion
  1.3 1.3 %pad.4 = s32[512]{0:T(512)} pad(s32[500]{0:T(512)} %param.15, s32[]{:T(128)} %constant.36.clone.1), padding=0_12 | pad | bytes 4052 | tf_op jit(solution)/shard_map/jit(_pad)/pad | solution.py:435
  2.6 0.1 iota_add_fusion
  2.6 0.1 add.33
  2.7 0.2 fusion.6
  3.0 0.6 maximum_maximum_fusion.mat
  3.6 1.7 %copy.11 = bf16[16,8,2,512]{3,1,2,0:T(8,128)(2,1)} copy(bf16[16,8,2,512]{3,2,1,0:T(2,128)(2,1)} %bitcast.7) | data formatting | bytes 524288
  5.3 98.0 %spectra.1 = (bf16[16,256,512]{2,1,0:T(8,128)(2,1)}, bf16[16,256,512]{2,1,0:T(8,128)(2,1)}, bf16[1024,512]{1,0:T(8,128)(2,1)}, bf16[512,512]{1,0:T(8,128)(2,1)}) custom-call(bf16[2,32,65536]{2,1,0:T(8,128)(2,1)} %volt.1, bf16[128,1024]{1,0:T(8,128)(2,1)} %bitcast.6, bf16[1024,1024]{1,0:T(8,128)(2,1)} %constant.41.clone.emat, f32[4,4096]{1,0:T(4,128)} %taps.1, ...), custom_call_target="tpu_custom_call" | custom-call | tf_op jit(solution)/shard_map/spectra/pallas_call | solution.py:389
  103.3 22.7 %products.1 = (f32[2,4,512,512]{3,2,1,0:T(8,128)}, bf16[2,500,16,128]{3,2,1,0:T(8,128)(2,1)}) custom-call(bf16[16,256,512]{2,1,0:T(8,128)(2,1)} %get-tuple-element.8.xt, bf16[16,256,512]{2,1,0:T(8,128)(2,1)} %get-tuple-element.9.ct, bf16[1024,512]{1,0:T(8,128)(2,1)} %get-tuple-element.10.weights, bf16[512,512]{1,0:T(8,128)(2,1)} %get-tuple-element.11.order), custom_call_target="tpu_custom_call" | custom-call | tf_op jit(solution)/shard_map/products/pallas_call | solution.py:494

commit v3 on v2

v3 whole, which is shorter than its diff:
```python
import functools
import math

import jax
import jax.numpy as jnp
import numpy as np
from jax import lax
from jax.experimental import pallas as pl
from jax.experimental.pallas import tpu as pltpu
from jax.sharding import PartitionSpec as P

LANES = 128
HALF = 16
BLOCKS = 32
ROWS = 80
PITCH = 81
MESH = pl.DeviceIdType.MESH


def twiddles():
    k = np.arange(BLOCKS)[:, None].astype(np.float64)
    lane = np.arange(LANES)[None, :].astype(np.float64)
    angle = 2.0 * np.pi / 4096.0 * k * lane
    return np.stack([np.cos(angle), -np.sin(angle)]).astype(np.float32)


def lane_table():
    bins = np.arange(LANES)
    angle = 2.0 * np.pi / LANES * (bins[:, None] * bins[None, :] % LANES)
    cosine, sine = np.cos(angle) / 64.0, np.sin(angle) / 64.0
    return np.block([[cosine, sine], [-sine, cosine]]).astype(np.float32)


def cmul_const(re, im, angle):
    c, s = math.cos(angle), math.sin(angle)
    if abs(s) < 1e-12 and c > 0:
        return re, im
    if abs(c) < 1e-12:
        return (im, -re) if s > 0 else (-im, re)
    if abs(abs(c) - abs(s)) < 1e-12 and c > 0 and s > 0:
        return (re + im) * c, (im - re) * c
    if abs(abs(c) - abs(s)) < 1e-12 and c < 0 and s > 0:
        return (im - re) * s, (im + re) * (-s)
    return re * c + im * s, im * c - re * s


def dft4(x):
    (ar, ai), (br, bi), (cr, ci), (dr, di) = x
    pr, pi = ar + cr, ai + ci
    qr, qi = ar - cr, ai - ci
    rr, ri = br + dr, bi + di
    sr, si = br - dr, bi - di
    return [
        (pr + rr, pi + ri),
        (qr + si, qi - sr),
        (pr - rr, pi - ri),
        (qr - si, qi + sr),
    ]


def dft8(x):
    even = dft4(x[0::2])
    odd = dft4(x[1::2])
    odd = [cmul_const(r, i, 2.0 * math.pi * k / 8.0) for k, (r, i) in enumerate(odd)]
    low = [(e[0] + o[0], e[1] + o[1]) for e, o in zip(even, odd)]
    high = [(e[0] - o[0], e[1] - o[1]) for e, o in zip(even, odd)]
    return low + high


NT = (((1,), (1,)), ((), ()))
TN = (((0,), (0,)), ((), ()))


def dot(a, b, dims=(((1,), (0,)), ((), ()))):
    return lax.dot_general(a, b, dims, preferred_element_type=jnp.float32)


def iota(shape, dim):
    return lax.broadcasted_iota(jnp.int32, shape, dim)


def one_hot(found):
    return jnp.where(found, 1.0, 0.0).astype(jnp.bfloat16)


def spectra_kernel(
    volt, steer, taps, tw, lines, bands, smap, beam, calib,
    xt, ct, weights, order,
    vbuf, stage, ybuf, tbuf, sbuf, rbuf, xin, res, ebuf, gains, table, wpart, wall, mat, bidx,
    load_sems, send_sems, recv_sems, steer_sems,
):
    me_c = lax.axis_index("chan")
    me_s = lax.axis_index("sect")
    n_c = lax.axis_size("chan")
    n_s = lax.axis_size("sect")
    count = n_c * n_s
    frames = volt.shape[2] // 4096
    core = lax.rem(me_c, 2)
    chip = me_c // 2
    my_x = lax.rem(chip, 2) * 2 + me_s // 4
    my_y = lax.rem(me_s, 4)
    my_z = chip // 2

    def load(half, f):
        return pltpu.make_async_copy(
            volt.at[:, pl.ds(half * HALF, HALF), pl.ds(f * 4096, 4096)],
            vbuf.at[half, f + 3],
            load_sems.at[half, f // 8],
        )

    for half in range(2):

        @pl.loop(0, frames)
        def _(f):
            load(half, f).start()

    barrier = pltpu.get_barrier_semaphore()

    @pl.loop(1, count)
    def _(step):
        c = lax.rem(me_c + step // n_s, n_c)
        s = lax.rem(me_s + lax.rem(step, n_s), n_s)
        pl.semaphore_signal(barrier, inc=1, device_id=(c, s), device_id_type=MESH)

    for half in range(2):
        for pad in range(3):
            vbuf[half, pad] = jnp.zeros(vbuf.shape[2:], vbuf.dtype)
            vbuf[half, frames + 3 + pad] = jnp.zeros(vbuf.shape[2:], vbuf.dtype)

    column = iota((32, LANES), 1)
    spread = one_hot(lax.rem(column, 64) // 2 == iota((32, LANES), 0))
    number = jnp.broadcast_to(bands[...] // 64, (8, 32)).astype(jnp.float32)
    column = iota((8, LANES), 1)
    wanted = dot(number.astype(jnp.bfloat16), spread).astype(jnp.int32) * 2
    wanted = wanted + lax.rem(column, 2) + column // 64 * LANES
    mat[...] = dot(
        one_hot(wanted[:1] == iota((2 * LANES, LANES), 0)), lines[...].astype(jnp.bfloat16), TN
    ).astype(jnp.bfloat16)
    bidx[...] = jnp.full(bidx.shape, -1, jnp.int32)
    bidx[:, : beam.shape[1]] = beam[...]

    pl.semaphore_wait(barrier, count - 1)

    mine = my_z * 2 + core
    share = steer.at[:, pl.ds(pl.multiple_of(mine * LANES, LANES), LANES)]

    @pl.loop(1, n_s)
    def _(step):
        pltpu.make_async_remote_copy(
            src_ref=share,
            dst_ref=table.at[me_s],
            send_sem=steer_sems.at[0],
            recv_sem=steer_sems.at[1],
            device_id=(me_c, lax.rem(me_s + step, n_s)),
            device_id_type=MESH,
        ).start()

    pltpu.make_async_copy(share, table.at[me_s], steer_sems.at[1]).start()

    def pick_and_share():
        pltpu.make_async_copy(table, table, steer_sems.at[1]).wait()
        total = None
        for s in range(8):
            found = bidx[...] == iota((LANES, 512), 0) + s * LANES
            term = dot(one_hot(found), table[s], TN)
            total = term if total is None else total + term
        wpart[...] = total.astype(jnp.bfloat16)

        @pl.loop(1, 4)
        def _(step):
            pltpu.make_async_remote_copy(
                src_ref=wpart,
                dst_ref=wall.at[mine],
                send_sem=steer_sems.at[2],
                recv_sem=steer_sems.at[3],
                device_id=(lax.rem(me_c + step * 4, n_c), me_s),
                device_id_type=MESH,
            ).start()

        pltpu.make_async_remote_copy(
            src_ref=wpart,
            dst_ref=wall.at[mine],
            send_sem=steer_sems.at[2],
            recv_sem=steer_sems.at[4],
            device_id=(me_c + 1 - 2 * core, me_s),
            device_id_type=MESH,
        ).start()
        pltpu.make_async_copy(wpart, wall.at[mine], steer_sems.at[3]).start()

    def pass_on():
        four = wall.at[pl.ds(0, 4)]
        pltpu.make_async_copy(four, four, steer_sems.at[3]).wait()

        @pl.loop(1, 4)
        def _(step):
            other = lax.rem(my_z + step, 4) * 2 + core
            pltpu.make_async_remote_copy(
                src_ref=wall.at[other],
                dst_ref=wall.at[other],
                send_sem=steer_sems.at[5],
                recv_sem=steer_sems.at[4],
                device_id=(me_c + 1 - 2 * core, me_s),
                device_id_type=MESH,
            ).start()

    def one_frame(half, f):
        for q0 in range(8):
            four = []
            for q1 in range(4):
                cols = pl.ds((q0 + 8 * q1) * LANES, LANES)
                parts = []
                for part in range(2):
                    total = None
                    for t in range(4):
                        x = vbuf[half, f + 3 - t, part, :, cols].astype(jnp.float32)
                        term = x * taps[t : t + 1, cols]
                        total = term if total is None else total + term
                    parts.append(total)
                four.append(tuple(parts))
            for ka, (re, im) in enumerate(dft4(four)):
                re, im = cmul_const(re, im, 2.0 * math.pi * q0 * ka / 32.0)
                stage[ka, q0, 0] = re
                stage[ka, q0, 1] = im
        for ka in range(4):
            eight = [(stage[ka, q0, 0], stage[ka, q0, 1]) for q0 in range(8)]
            for kb, (re, im) in enumerate(dft8(eight)):
                k = ka + 4 * kb
                c = tw[0, k : k + 1, :]
                s = tw[1, k : k + 1, :]
                rows = pl.ds(k * HALF, HALF)
                ybuf[rows, :LANES] = (re * c - im * s).astype(jnp.bfloat16)
                ybuf[rows, LANES:] = (re * s + im * c).astype(jnp.bfloat16)
        own = f < frames
        for group in range(4):
            k_hi, kh = group // 2, group % 2
            out = dot(mat[...], ybuf[group * LANES : (group + 1) * LANES, :], NT)
            for part in range(2):
                base = k_hi * 64 * PITCH + jnp.where(
                    own,
                    f // 8 * 48 + kh * 16 + part * 8 + lax.rem(f, 8),
                    32 + kh * 8 + part * 4 + f - frames,
                )
                tbuf[pl.ds(base, 64, stride=PITCH), :] = out[part * 64 : (part + 1) * 64]

    slot = me_s * n_c + me_c

    def message_rows(half, late):
        cut = 48 if half else 32
        return pl.ds(cut, ROWS - cut) if late else pl.ds(0, cut)

    def send_out(half, late):
        rows = message_rows(half, late)

        @pl.loop(0, count // 2)
        def _(step):
            k0 = lax.rem(step, 4)
            k1 = lax.rem(step // 4, 4)
            k2 = step // 16
            x = lax.rem(my_x + k0, 4)
            y = lax.rem(my_y + k0 + k1, 4)
            z = lax.rem(my_z + k0 + k1 + k2, 4)
            for flip in range(2):
                c = (z * 2 + x // 2) * 2 + lax.rem(core + flip, 2)
                s = lax.rem(x, 2) * 4 + y
                dest = c * n_s + s
                first = (lax.rem(dest, 2) * 64 + dest // 2) * PITCH + rows.start
                block = tbuf[pl.ds(first, rows.size), :]
                sbuf[half, dest, rows] = block.astype(jnp.bfloat16)

                def go():
                    pltpu.make_async_remote_copy(
                        src_ref=sbuf.at[half, dest, rows],
                        dst_ref=rbuf.at[half, slot, rows],
                        send_sem=send_sems.at[half, late],
                        recv_sem=recv_sems.at[half, late],
                        device_id=(c, s),
                        device_id_type=MESH,
                    ).start()

                if flip:
                    go()
                else:
                    pl.when(step > 0)(go)

                    @pl.when(step == 0)
                    def _():
                        pltpu.make_async_copy(
                            sbuf.at[half, dest, rows],
                            rbuf.at[half, slot, rows],
                            recv_sems.at[half, late],
                        ).start()

    def arrived(half, late):
        part = vbuf.at[half, pl.ds(3 + 8 * late, 8)]
        pltpu.make_async_copy(part, part, load_sems.at[half, late]).wait()

    arrived(0, 0)

    @pl.loop(0, 8)
    def _(f):
        one_frame(0, f)

    send_out(0, 0)
    pick_and_share()
    arrived(0, 1)

    @pl.loop(8, frames + 3)
    def _(f):
        one_frame(0, f)

    send_out(0, 1)
    pass_on()
    arrived(1, 0)
    arrived(1, 1)

    @pl.loop(0, 11)
    def _(i):
        one_frame(1, jnp.where(i < 8, i, i + 8))

    send_out(1, 0)

    @pl.loop(8, frames)
    def _(f):
        one_frame(1, f)

    send_out(1, 1)

    rank = iota((512, 512), 1)
    natural = lax.rem(rank // 16, 16) * 32 + rank // 256 * 16 + lax.rem(rank, 16)
    move = one_hot(iota((512, 512), 0) == natural)
    order[...] = dot(one_hot(smap[...] == iota((512, 512), 0)), move).astype(jnp.bfloat16)
    gains[...] = dot(calib[...], order[...])
    line = iota((1024, 1024), 1)
    source = lax.rem(line // 16, 8) * LANES + line // LANES * 16 + lax.rem(line, 16)
    ebuf[...] = one_hot(iota((1024, 1024), 0) == source)
    four = wall.at[pl.ds(0, 4)]
    pltpu.make_async_copy(four, four, steer_sems.at[4]).wait()
    for part in range(2):
        picked = jnp.concatenate([wall[part * 4 + j] for j in range(4)], axis=1)
        weights[part * 512 : (part + 1) * 512, :] = dot(picked, order[...]).astype(jnp.bfloat16)

    row = iota((8, LANES), 0)
    for half in range(2):
        for late in range(2):
            rows = message_rows(half, late)
            pltpu.make_async_copy(
                rbuf.at[half, :, rows], rbuf.at[half, :, rows], recv_sems.at[half, late]
            ).wait()
            if late < 1 - half:
                continue
            for fh in (late,) if half else (0, 1):
                for kh in range(2):
                    for c_hi in range(2):
                        at_row = (kh * 2 + c_hi) * LANES

                        @pl.loop(0, n_s)
                        def _(s):
                            before = jnp.maximum(s - 1, 0)
                            keep = (row < 3) & (s > 0)
                            there = pl.ds(pl.multiple_of(at_row + s * 16, 16), 16)
                            for c_lo in range(8):
                                c = c_hi * 8 + c_lo
                                lanes = slice(c_lo * LANES, (c_lo + 1) * LANES)
                                at = fh * 48 + kh * 16
                                piece = rbuf[half, s * n_c + c, at : at + 16]
                                if fh == 0:
                                    extra = rbuf[half, before * n_c + c, 32:48]
                                    extra = extra.astype(jnp.float32)[kh * 8 : kh * 8 + 8]
                                    extra = jnp.concatenate(
                                        [
                                            jnp.where(keep, extra, 0.0),
                                            jnp.where(keep, pltpu.roll(extra, 4, 0), 0.0),
                                        ],
                                        axis=0,
                                    )
                                    piece = piece.astype(jnp.float32) + extra
                                xin[there, lanes] = piece.astype(jnp.bfloat16)

                res[fh] = dot(xin[...], ebuf[...])

        for kh in range(2):
            for c_hi in range(2):
                cols = slice(half * 256 + c_hi * LANES, half * 256 + (c_hi + 1) * LANES)
                at_row = (kh * 2 + c_hi) * LANES

                @pl.loop(0, n_s)
                def _(s):
                    low = pl.ds(pl.multiple_of(s * 16, 16), 16)
                    high = pl.ds(pl.multiple_of(128 + s * 16, 16), 16)
                    first = pl.ds(pl.multiple_of(at_row + s * 16, 8), 8)
                    second = pl.ds(pl.multiple_of(at_row + s * 16 + 8, 8), 8)
                    for k8 in range(8):
                        ch = kh * 8 + k8
                        lanes = slice(k8 * LANES, (k8 + 1) * LANES)
                        real = jnp.concatenate([res[0, first, lanes], res[1, first, lanes]], axis=0)
                        imag = jnp.concatenate(
                            [res[0, second, lanes], res[1, second, lanes]], axis=0
                        )
                        xt[ch, low, cols] = real.astype(jnp.bfloat16)
                        xt[ch, high, cols] = imag.astype(jnp.bfloat16)
                        g_re = gains[ch : ch + 1, cols]
                        g_im = gains[16 + ch : 17 + ch, cols]
                        ct[ch, low, cols] = (g_re * real - g_im * imag).astype(jnp.bfloat16)
                        ct[ch, high, cols] = (g_re * imag + g_im * real).astype(jnp.bfloat16)

    for half in range(2):
        for late in range(2):
            sent = sbuf.at[half, pl.ds(0, count - 1), message_rows(half, late)]
            pltpu.make_async_copy(sent, sent, send_sems.at[half, late]).wait()
    sent = table.at[pl.ds(0, 7)]
    pltpu.make_async_copy(sent, sent, steer_sems.at[0]).wait()
    sent = wall.at[pl.ds(0, 4)]
    pltpu.make_async_copy(sent, sent, steer_sems.at[2]).wait()
    sent = wall.at[pl.ds(0, 3)]
    pltpu.make_async_copy(sent, sent, steer_sems.at[5]).wait()


def channelize(voltages, fir_taps, band_start, steer, station_map, beam_index, calib):
    count = lax.axis_size("chan") * lax.axis_size("sect")
    frames = voltages.shape[2] // 4096
    hbm = pl.BlockSpec(memory_space=pl.ANY)
    vmem = pl.BlockSpec(memory_space=pltpu.VMEM)
    half16 = jnp.bfloat16
    return pl.pallas_call(
        spectra_kernel,
        out_shape=(
            pltpu.VMEM((16, 256, 512), half16),
            pltpu.VMEM((16, 256, 512), half16),
            pltpu.VMEM((1024, 512), half16),
            pltpu.VMEM((512, 512), half16),
        ),
        in_specs=[hbm] * 2 + [vmem] * 7,
        out_specs=(vmem,) * 4,
        scratch_shapes=[
            pltpu.VMEM((2, frames + 6, 2, HALF, 4096), half16),
            pltpu.VMEM((4, 8, 2, HALF, LANES), jnp.float32),
            pltpu.VMEM((BLOCKS * HALF, 2 * LANES), half16),
            pltpu.VMEM((count * PITCH, LANES), jnp.float32),
            pltpu.VMEM((2, count, ROWS, LANES), half16),
            pltpu.VMEM((2, count, ROWS, LANES), half16),
            pltpu.VMEM((512, 1024), half16),
            pltpu.VMEM((2, 512, 1024), jnp.float32),
            pltpu.VMEM((1024, 1024), half16),
            pltpu.VMEM((32, 512), jnp.float32),
            pltpu.VMEM((8, LANES, LANES), half16),
            pltpu.VMEM((512, LANES), half16),
            pltpu.VMEM((8, 512, LANES), half16),
            pltpu.VMEM((LANES, 2 * LANES), half16),
            pltpu.VMEM((1, 512), jnp.int32),
            pltpu.SemaphoreType.DMA((2, 2)),
            pltpu.SemaphoreType.DMA((2, 2)),
            pltpu.SemaphoreType.DMA((2, 2)),
            pltpu.SemaphoreType.DMA((6,)),
        ],
        compiler_params=pltpu.CompilerParams(
            collective_id=0, has_side_effects=True, vmem_limit_bytes=48 * 1024 * 1024
        ),
        name="spectra",
    )(
        voltages,
        steer.reshape(LANES, 1024),
        fir_taps,
        jnp.asarray(twiddles()),
        jnp.asarray(lane_table()),
        band_start.reshape(1, 32),
        station_map.reshape(1, 512),
        beam_index.reshape(1, -1),
        calib.reshape(32, 512),
    )


def product_kernel(
    scale, xt, ct, weights, order, vis, beams, zbuf, wbuf, bbuf, obuf, pbuf, beam_sems, vis_sems
):
    n_b = beams.shape[1]
    tiles = bbuf.shape[0]

    @pl.loop(0, xt.shape[0])
    def _(ch):
        uv = dot(weights[...], ct[ch], NT)
        real = uv[:512, :128] - uv[512:, 128:]
        imag = uv[:512, 128:] + uv[512:, :128]
        both = jnp.concatenate([real, imag], axis=1).astype(jnp.bfloat16)
        rows = pl.ds(pl.multiple_of(ch * 16, 16), 16)
        bbuf[:, rows, :] = both.reshape(tiles, 16, 256)

    line = iota((256, 256), 0)
    source = lax.rem(line, 16) * 16 + line // 16
    move = one_hot(iota((256, 256), 1) == source)

    @pl.loop(0, tiles // 4)
    def _(four):
        for j in range(4):
            tile = four * 4 + j
            out = dot(move, bbuf[tile]).astype(jnp.bfloat16)
            for part in range(2):
                piece = out[:, part * 128 : (part + 1) * 128].reshape(16, 16, 128)
                obuf[part, pl.ds(tile * 16, 16)] = piece

    def put_beams(part):
        return pltpu.make_async_copy(
            obuf.at[part, pl.ds(0, n_b)], beams.at[part], beam_sems.at[part]
        )

    def put_vis(part, g):
        return pltpu.make_async_copy(pbuf.at[part, g % 2], vis.at[part, g], vis_sems.at[part, g % 2])

    for part in range(2):
        put_beams(part).start()

    for g in range(4):
        for a in range(4):
            z = dot(order[...], xt[g * 4 + a], NT).astype(jnp.bfloat16)
            zbuf[:, a * 256 : (a + 1) * 256] = z
            wbuf[:, a * 256 : a * 256 + 128] = z[:, 128:]
            wbuf[:, a * 256 + 128 : (a + 1) * 256] = -z[:, :128]
        for part, left in enumerate((zbuf, wbuf)):
            if g >= 2:
                put_vis(part, g - 2).wait()
            pbuf[part, g % 2] = dot(left[...], zbuf[...], NT) * scale
            put_vis(part, g).start()

    for part in range(2):
        for g in (2, 3):
            put_vis(part, g).wait()
        put_beams(part).wait()


def products(xt, ct, weights, order):
    half16 = jnp.bfloat16
    hbm = pl.BlockSpec(memory_space=pl.ANY)
    vmem = pl.BlockSpec(memory_space=pltpu.VMEM)
    vis, beams = pl.pallas_call(
        functools.partial(product_kernel, 1.0 / 512.0),
        out_shape=(
            jax.ShapeDtypeStruct((2, 4, 512, 512), jnp.float32),
            jax.ShapeDtypeStruct((2, 500, 16, 128), half16),
        ),
        in_specs=[vmem] * 4,
        out_specs=(hbm, hbm),
        scratch_shapes=[
            pltpu.VMEM((512, 1024), half16),
            pltpu.VMEM((512, 1024), half16),
            pltpu.VMEM((32, 256, 256), half16),
            pltpu.VMEM((2, 512, 16, 128), half16),
            pltpu.VMEM((2, 2, 512, 512), jnp.float32),
            pltpu.SemaphoreType.DMA((2,)),
            pltpu.SemaphoreType.DMA((2, 2)),
        ],
        compiler_params=pltpu.CompilerParams(vmem_limit_bytes=40 * 1024 * 1024),
        name="products",
    )(xt, ct, weights, order)
    return vis, jnp.transpose(beams, (0, 2, 1, 3))


def shards(voltages, fir_taps, station_map, band_start, calib, steer, beam_index):
    parts = channelize(
        voltages, fir_taps, band_start, steer, station_map, beam_index, calib
    )
    return products(*parts)


def solution(mesh):
    return jax.shard_map(
        shards,
        mesh=mesh,
        in_specs=(
            P(None, "chan", "sect"),
            P(),
            P(),
            P(),
            P(None, ("chan", "sect"), None),
            P("sect", None, None),
            P(),
        ),
        out_specs=(P(None, ("chan", "sect"), None, None), P(None, ("chan", "sect"), None, None)),
        check_vma=False,
    )
```

time: 126 us -> 119 us (0.944)
  Pallas kernels: 121 us -> 116 us
  other arithmetic: 1.6 us -> 0 us
  local copies, waits for them, and re-layouts: 3.05 us -> 1.69 us
    pallas_call x2, Pallas kernels: 121 us -> 116 us  [the longest x1 97.2 us: channelize(): pl.pallas_call(spectra_kernel, out_shape=(pltpu.VMEM((16, 256, 512), half...]
    pad x1 -> x0, local copies, waits for them, and re-layouts: 1.26 us -> none  [channelize(): jnp.pad(beam_index, (0, 12), constant_values=-1).reshape(1, 512)]
where the time goes in v3:
time: 119 us; the launch traced here: 118 us
  Pallas kernels  116 us (97%)
  local copies, waits for them, and re-layouts  1.69 us (1%)
    pallas_call x1, Pallas kernels, channelize(): pl.pallas_call(spectra_kernel, out_shape=(pltpu.VMEM((16, 256, 512), half...  97.2 us
    pallas_call x1, Pallas kernels, products(): pl.pallas_call(functools.partial(product_kernel, 1.0 / 512.0), out_shape=...  18.6 us

profile of v3, /device:TPU:1, one launch (start us, length us, event | category | flops | bytes accessed | tf_op | source)
XLA Modules:
  0.0 118.4 jit_solution(6875149838976347819)
XLA Ops:
  0.6 1.7 %copy.11 = bf16[16,8,2,512]{3,1,2,0:T(8,128)(2,1)} copy(bf16[16,8,2,512]{3,2,1,0:T(2,128)(2,1)} %bitcast.8) | data formatting | bytes 524288
  2.3 97.2 %spectra.1 = (bf16[16,256,512]{2,1,0:T(8,128)(2,1)S(1)}, bf16[16,256,512]{2,1,0:T(8,128)(2,1)S(1)}, bf16[1024,512]{1,0:T(8,128)(2,1)S(1)}, bf16[512,512]{1,0:T(8,128)(2,1)S(1)}) custom-call(bf16[2,32,65536]{2,1,0:T(8,128)(2,1)} %volt.1, bf16[128,1024]{1,0:T(8,128)(2,1)} %bitcast.7, f32[4,4096]{1,0:T(4,128)} %taps.1, f32[2,32,128]{2,1,0:T(8,128)} %constant.4.clone.tw, ...), custom_call_target="tpu_custom_call" | custom-call | tf_op jit(solution)/shard_map/spectra/pallas_call | solution.py:424
  99.6 18.6 %products.1 = (f32[2,4,512,512]{3,2,1,0:T(8,128)}, bf16[2,500,16,128]{3,2,1,0:T(8,128)(2,1)}) custom-call(bf16[16,256,512]{2,1,0:T(8,128)(2,1)S(1)} %get-tuple-element.8.xt, bf16[16,256,512]{2,1,0:T(8,128)(2,1)S(1)} %get-tuple-element.9.ct, bf16[1024,512]{1,0:T(8,128)(2,1)S(1)} %get-tuple-element.10.weights, bf16[512,512]{1,0:T(8,128)(2,1)S(1)} %get-tuple-element.11.order), custom_call_target="tpu_custom_call" | custom-call | tf_op jit(solution)/shard_map/products/pallas_call | solution.py:533

commit v4 on v3

--- a/solution.py
+++ b/solution.py
@@ -87,6 +87,7 @@
     volt, steer, taps, tw, lines, bands, smap, beam, calib,
     xt, ct, weights, order,
     vbuf, stage, ybuf, tbuf, sbuf, rbuf, xin, res, ebuf, gains, table, wpart, wall, mat, bidx,
+    pick,
     load_sems, send_sems, recv_sems, steer_sems,
 ):
     me_c = lax.axis_index("chan")
@@ -140,7 +141,6 @@
     bidx[:, : beam.shape[1]] = beam[...]
 
     pl.semaphore_wait(barrier, count - 1)
-
     mine = my_z * 2 + core
     share = steer.at[:, pl.ds(pl.multiple_of(mine * LANES, LANES), LANES)]
 
@@ -157,14 +157,14 @@
 
     pltpu.make_async_copy(share, table.at[me_s], steer_sems.at[1]).start()
 
+    entry = jnp.broadcast_to(bidx[...].astype(jnp.float32), (LANES, 512)).T
+    entry = entry.astype(jnp.int32)
+    for s in range(8):
+        pick[:, s * LANES : (s + 1) * LANES] = one_hot(entry == iota((512, LANES), 1) + s * LANES)
+
     def pick_and_share():
         pltpu.make_async_copy(table, table, steer_sems.at[1]).wait()
-        total = None
-        for s in range(8):
-            found = bidx[...] == iota((LANES, 512), 0) + s * LANES
-            term = dot(one_hot(found), table[s], TN)
-            total = term if total is None else total + term
-        wpart[...] = total.astype(jnp.bfloat16)
+        wpart[...] = dot(pick[...], table[...].reshape(8 * LANES, LANES)).astype(jnp.bfloat16)
 
         @pl.loop(1, 4)
         def _(step):
@@ -251,7 +251,7 @@
     def send_out(half, late):
         rows = message_rows(half, late)
 
-        @pl.loop(0, count // 2)
+        @pl.loop(0, count // 2, unroll=2)
         def _(step):
             k0 = lax.rem(step, 4)
             k1 = lax.rem(step // 4, 4)
@@ -296,12 +296,17 @@
 
     arrived(0, 0)
 
-    @pl.loop(0, 8)
+    @pl.loop(0, 3)
     def _(f):
         one_frame(0, f)
 
+    pick_and_share()
+
+    @pl.loop(3, 8)
+    def _(f):
+        one_frame(0, f)
+
     send_out(0, 0)
-    pick_and_share()
     arrived(0, 1)
 
     @pl.loop(8, frames + 3)
@@ -447,6 +452,7 @@
             pltpu.VMEM((8, 512, LANES), half16),
             pltpu.VMEM((LANES, 2 * LANES), half16),
             pltpu.VMEM((1, 512), jnp.int32),
+            pltpu.VMEM((512, 1024), half16),
             pltpu.SemaphoreType.DMA((2, 2)),
             pltpu.SemaphoreType.DMA((2, 2)),
             pltpu.SemaphoreType.DMA((2, 2)),
@@ -475,7 +481,7 @@
     n_b = beams.shape[1]
     tiles = bbuf.shape[0]
 
-    @pl.loop(0, xt.shape[0])
+    @pl.loop(0, xt.shape[0], unroll=4)
     def _(ch):
         uv = dot(weights[...], ct[ch], NT)
         real = uv[:512, :128] - uv[512:, 128:]
@@ -488,7 +494,7 @@
     source = lax.rem(line, 16) * 16 + line // 16
     move = one_hot(iota((256, 256), 1) == source)
 
-    @pl.loop(0, tiles // 4)
+    @pl.loop(0, tiles // 4, unroll=2)
     def _(four):
         for j in range(4):
             tile = four * 4 + j

time: 119 us -> 124 us (1.042)
  Pallas kernels: 116 us -> 121 us
    pallas_call x1, Pallas kernels: 97.2 us -> 106 us  [channelize(): pl.pallas_call(spectra_kernel, out_shape=(pltpu.VMEM((16, 256, 512), half...]
    pallas_call x1, Pallas kernels: 18.6 us -> 15.7 us  [products(): pl.pallas_call(functools.partial(product_kernel, 1.0 / 512.0), out_shape=...]
where the time goes in v4:
time: 124 us
  Pallas kernels  121 us (98%)
  local copies, waits for them, and re-layouts  1.69 us (1%)
    pallas_call x1, Pallas kernels, channelize(): pl.pallas_call(spectra_kernel, out_shape=(pltpu.VMEM((16, 256, 512), half...  106 us
    pallas_call x1, Pallas kernels, products(): pl.pallas_call(functools.partial(product_kernel, 1.0 / 512.0), out_shape=...  15.7 us

profile of v4, /device:TPU:1, one launch (start us, length us, event | category | flops | bytes accessed | tf_op | source)
XLA Modules:
  0.0 123.9 jit_solution(16086897578896804572)
XLA Ops:
  0.6 1.7 %copy.11 = bf16[16,8,2,512]{3,1,2,0:T(8,128)(2,1)} copy(bf16[16,8,2,512]{3,2,1,0:T(2,128)(2,1)} %bitcast.8) | data formatting | bytes 524288
  2.3 105.6 %spectra.1 = (bf16[16,256,512]{2,1,0:T(8,128)(2,1)S(1)}, bf16[16,256,512]{2,1,0:T(8,128)(2,1)S(1)}, bf16[1024,512]{1,0:T(8,128)(2,1)S(1)}, bf16[512,512]{1,0:T(8,128)(2,1)S(1)}) custom-call(bf16[2,32,65536]{2,1,0:T(8,128)(2,1)} %volt.1, bf16[128,1024]{1,0:T(8,128)(2,1)} %bitcast.7, f32[4,4096]{1,0:T(4,128)} %taps.1, f32[2,32,128]{2,1,0:T(8,128)} %constant.4.clone.tw, ...), custom_call_target="tpu_custom_call" | custom-call | tf_op jit(solution)/shard_map/spectra/pallas_call | solution.py:429
  108.0 15.7 %products.1 = (f32[2,4,512,512]{3,2,1,0:T(8,128)}, bf16[2,500,16,128]{3,2,1,0:T(8,128)(2,1)}) custom-call(bf16[16,256,512]{2,1,0:T(8,128)(2,1)S(1)} %get-tuple-element.8.xt, bf16[16,256,512]{2,1,0:T(8,128)(2,1)S(1)} %get-tuple-element.9.ct, bf16[1024,512]{1,0:T(8,128)(2,1)S(1)} %get-tuple-element.10.weights, bf16[512,512]{1,0:T(8,128)(2,1)S(1)} %get-tuple-element.11.order), custom_call_target="tpu_custom_call" | custom-call | tf_op jit(solution)/shard_map/products/pallas_call | solution.py:539

commit v5 on v4

--- a/solution.py
+++ b/solution.py
@@ -101,6 +101,7 @@
     my_x = lax.rem(chip, 2) * 2 + me_s // 4
     my_y = lax.rem(me_s, 4)
     my_z = chip // 2
+    mine = my_z * 2 + core
 
     def load(half, f):
         return pltpu.make_async_copy(
@@ -123,10 +124,11 @@
         s = lax.rem(me_s + lax.rem(step, n_s), n_s)
         pl.semaphore_signal(barrier, inc=1, device_id=(c, s), device_id_type=MESH)
 
-    for half in range(2):
+    def clear(half, first):
         for pad in range(3):
-            vbuf[half, pad] = jnp.zeros(vbuf.shape[2:], vbuf.dtype)
-            vbuf[half, frames + 3 + pad] = jnp.zeros(vbuf.shape[2:], vbuf.dtype)
+            vbuf[half, first + pad] = jnp.zeros(vbuf.shape[2:], vbuf.dtype)
+
+    clear(0, 0)
 
     column = iota((32, LANES), 1)
     spread = one_hot(lax.rem(column, 64) // 2 == iota((32, LANES), 0))
@@ -140,30 +142,29 @@
     bidx[...] = jnp.full(bidx.shape, -1, jnp.int32)
     bidx[:, : beam.shape[1]] = beam[...]
 
-    pl.semaphore_wait(barrier, count - 1)
-    mine = my_z * 2 + core
-    share = steer.at[:, pl.ds(pl.multiple_of(mine * LANES, LANES), LANES)]
-
-    @pl.loop(1, n_s)
-    def _(step):
-        pltpu.make_async_remote_copy(
-            src_ref=share,
-            dst_ref=table.at[me_s],
-            send_sem=steer_sems.at[0],
-            recv_sem=steer_sems.at[1],
-            device_id=(me_c, lax.rem(me_s + step, n_s)),
-            device_id_type=MESH,
-        ).start()
-
-    pltpu.make_async_copy(share, table.at[me_s], steer_sems.at[1]).start()
-
-    entry = jnp.broadcast_to(bidx[...].astype(jnp.float32), (LANES, 512)).T
-    entry = entry.astype(jnp.int32)
-    for s in range(8):
-        pick[:, s * LANES : (s + 1) * LANES] = one_hot(entry == iota((512, LANES), 1) + s * LANES)
+    def share_table():
+        share = steer.at[:, pl.ds(pl.multiple_of(mine * LANES, LANES), LANES)]
+
+        @pl.loop(1, n_s)
+        def _(step):
+            pltpu.make_async_remote_copy(
+                src_ref=share,
+                dst_ref=table.at[me_s],
+                send_sem=steer_sems.at[0],
+                recv_sem=steer_sems.at[1],
+                device_id=(me_c, lax.rem(me_s + step, n_s)),
+                device_id_type=MESH,
+            ).start()
+
+        pltpu.make_async_copy(share, table.at[me_s], steer_sems.at[1]).start()
 
     def pick_and_share():
         pltpu.make_async_copy(table, table, steer_sems.at[1]).wait()
+        entry = jnp.broadcast_to(bidx[...].astype(jnp.float32), (LANES, 512)).T
+        entry = entry.astype(jnp.int32)
+        for s in range(8):
+            found = entry == iota((512, LANES), 1) + s * LANES
+            pick[:, s * LANES : (s + 1) * LANES] = one_hot(found)
         wpart[...] = dot(pick[...], table[...].reshape(8 * LANES, LANES)).astype(jnp.bfloat16)
 
         @pl.loop(1, 4)
@@ -251,7 +252,7 @@
     def send_out(half, late):
         rows = message_rows(half, late)
 
-        @pl.loop(0, count // 2, unroll=2)
+        @pl.loop(0, count // 2)
         def _(step):
             k0 = lax.rem(step, 4)
             k1 = lax.rem(step // 4, 4)
@@ -296,17 +297,16 @@
 
     arrived(0, 0)
 
-    @pl.loop(0, 3)
+    @pl.loop(0, 8)
     def _(f):
         one_frame(0, f)
 
-    pick_and_share()
-
-    @pl.loop(3, 8)
-    def _(f):
-        one_frame(0, f)
-
+    pl.semaphore_wait(barrier, count - 1)
     send_out(0, 0)
+    share_table()
+    clear(0, frames + 3)
+    clear(1, 0)
+    clear(1, frames + 3)
     arrived(0, 1)
 
     @pl.loop(8, frames + 3)
@@ -314,7 +314,7 @@
         one_frame(0, f)
 
     send_out(0, 1)
-    pass_on()
+    pick_and_share()
     arrived(1, 0)
     arrived(1, 1)
 
@@ -329,6 +329,7 @@
         one_frame(1, f)
 
     send_out(1, 1)
+    pass_on()
 
     rank = iota((512, 512), 1)
     natural = lax.rem(rank // 16, 16) * 32 + rank // 256 * 16 + lax.rem(rank, 16)

time: 124 us -> 111 us (0.90)
  Pallas kernels: 121 us -> 108 us
    pallas_call x1, Pallas kernels: 106 us -> 92.1 us  [channelize(): pl.pallas_call(spectra_kernel, out_shape=(pltpu.VMEM((16, 256, 512), half...]
where the time goes in v5:
time: 111 us; the launch traced here: 110 us
  Pallas kernels  108 us (97%)
  local copies, waits for them, and re-layouts  1.69 us (2%)
    pallas_call x1, Pallas kernels, channelize(): pl.pallas_call(spectra_kernel, out_shape=(pltpu.VMEM((16, 256, 512), half...  92.1 us
    pallas_call x1, Pallas kernels, products(): pl.pallas_call(functools.partial(product_kernel, 1.0 / 512.0), out_shape=...  15.7 us

profile of v5, /device:TPU:1, one launch (start us, length us, event | category | flops | bytes accessed | tf_op | source)
XLA Modules:
  0.0 110.3 jit_solution(2293921388553384568)
XLA Ops:
  0.6 1.7 %copy.11 = bf16[16,8,2,512]{3,1,2,0:T(8,128)(2,1)} copy(bf16[16,8,2,512]{3,2,1,0:T(2,128)(2,1)} %bitcast.8) | data formatting | bytes 524288
  2.3 92.1 %spectra.1 = (bf16[16,256,512]{2,1,0:T(8,128)(2,1)S(1)}, bf16[16,256,512]{2,1,0:T(8,128)(2,1)S(1)}, bf16[1024,512]{1,0:T(8,128)(2,1)S(1)}, bf16[512,512]{1,0:T(8,128)(2,1)S(1)}) custom-call(bf16[2,32,65536]{2,1,0:T(8,128)(2,1)} %volt.1, bf16[128,1024]{1,0:T(8,128)(2,1)} %bitcast.7, f32[4,4096]{1,0:T(4,128)} %taps.1, f32[2,32,128]{2,1,0:T(8,128)} %constant.4.clone.tw, ...), custom_call_target="tpu_custom_call" | custom-call | tf_op jit(solution)/shard_map/spectra/pallas_call | solution.py:430
  94.4 15.7 %products.1 = (f32[2,4,512,512]{3,2,1,0:T(8,128)}, bf16[2,500,16,128]{3,2,1,0:T(8,128)(2,1)}) custom-call(bf16[16,256,512]{2,1,0:T(8,128)(2,1)S(1)} %get-tuple-element.8.xt, bf16[16,256,512]{2,1,0:T(8,128)(2,1)S(1)} %get-tuple-element.9.ct, bf16[1024,512]{1,0:T(8,128)(2,1)S(1)} %get-tuple-element.10.weights, bf16[512,512]{1,0:T(8,128)(2,1)S(1)} %get-tuple-element.11.order), custom_call_target="tpu_custom_call" | custom-call | tf_op jit(solution)/shard_map/products/pallas_call | solution.py:540

commit v6 on v5

--- a/solution.py
+++ b/solution.py
@@ -110,11 +110,9 @@
             load_sems.at[half, f // 8],
         )
 
-    for half in range(2):
-
-        @pl.loop(0, frames)
-        def _(f):
-            load(half, f).start()
+    @pl.loop(0, 8)
+    def _(f):
+        load(0, f).start()
 
     barrier = pltpu.get_barrier_semaphore()
 
@@ -124,8 +122,16 @@
         s = lax.rem(me_s + lax.rem(step, n_s), n_s)
         pl.semaphore_signal(barrier, inc=1, device_id=(c, s), device_id_type=MESH)
 
+    @pl.loop(8, frames)
+    def _(f):
+        load(0, f).start()
+
+    @pl.loop(0, frames)
+    def _(f):
+        load(1, f).start()
+
     def clear(half, first):
-        for pad in range(3):
+        for pad in range(4 if first else 3):
             vbuf[half, first + pad] = jnp.zeros(vbuf.shape[2:], vbuf.dtype)
 
     clear(0, 0)
@@ -204,26 +210,36 @@
                 device_id_type=MESH,
             ).start()
 
-    def one_frame(half, f):
+    def frame_pair(half, f0):
         for q0 in range(8):
-            four = []
+            four = ([], [])
             for q1 in range(4):
                 cols = pl.ds((q0 + 8 * q1) * LANES, LANES)
-                parts = []
+                tap = [taps[t : t + 1, cols] for t in range(4)]
+                parts = ([], [])
                 for part in range(2):
-                    total = None
-                    for t in range(4):
-                        x = vbuf[half, f + 3 - t, part, :, cols].astype(jnp.float32)
-                        term = x * taps[t : t + 1, cols]
-                        total = term if total is None else total + term
-                    parts.append(total)
-                four.append(tuple(parts))
-            for ka, (re, im) in enumerate(dft4(four)):
-                re, im = cmul_const(re, im, 2.0 * math.pi * q0 * ka / 32.0)
-                stage[ka, q0, 0] = re
-                stage[ka, q0, 1] = im
+                    x = [
+                        vbuf[half, f0 + 4 - t, part, :, cols].astype(jnp.float32) for t in range(5)
+                    ]
+                    for which in range(2):
+                        total = None
+                        for t in range(4):
+                            term = x[t + 1 - which] * tap[t]
+                            total = term if total is None else total + term
+                        parts[which].append(total)
+                for which in range(2):
+                    four[which].append(tuple(parts[which]))
+            for which in range(2):
+                for ka, (re, im) in enumerate(dft4(four[which])):
+                    re, im = cmul_const(re, im, 2.0 * math.pi * q0 * ka / 32.0)
+                    stage[which, ka, q0, 0] = re
+                    stage[which, ka, q0, 1] = im
+        for which in range(2):
+            finish(f0 + which, which)
+
+    def finish(f, which):
         for ka in range(4):
-            eight = [(stage[ka, q0, 0], stage[ka, q0, 1]) for q0 in range(8)]
+            eight = [(stage[which, ka, q0, 0], stage[which, ka, q0, 1]) for q0 in range(8)]
             for kb, (re, im) in enumerate(dft8(eight)):
                 k = ka + 4 * kb
                 c = tw[0, k : k + 1, :]
@@ -297,9 +313,9 @@
 
     arrived(0, 0)
 
-    @pl.loop(0, 8)
-    def _(f):
-        one_frame(0, f)
+    @pl.loop(0, 4)
+    def _(i):
+        frame_pair(0, 2 * i)
 
     pl.semaphore_wait(barrier, count - 1)
     send_out(0, 0)
@@ -309,24 +325,24 @@
     clear(1, frames + 3)
     arrived(0, 1)
 
-    @pl.loop(8, frames + 3)
-    def _(f):
-        one_frame(0, f)
+    @pl.loop(4, 10)
+    def _(i):
+        frame_pair(0, 2 * i)
 
     send_out(0, 1)
     pick_and_share()
     arrived(1, 0)
     arrived(1, 1)
 
-    @pl.loop(0, 11)
+    @pl.loop(0, 6)
     def _(i):
-        one_frame(1, jnp.where(i < 8, i, i + 8))
+        frame_pair(1, 2 * jnp.where(i < 4, i, i + 4))
 
     send_out(1, 0)
 
-    @pl.loop(8, frames)
-    def _(f):
-        one_frame(1, f)
+    @pl.loop(4, 8)
+    def _(i):
+        frame_pair(1, 2 * i)
 
     send_out(1, 1)
     pass_on()
@@ -438,8 +454,8 @@
         in_specs=[hbm] * 2 + [vmem] * 7,
         out_specs=(vmem,) * 4,
         scratch_shapes=[
-            pltpu.VMEM((2, frames + 6, 2, HALF, 4096), half16),
-            pltpu.VMEM((4, 8, 2, HALF, LANES), jnp.float32),
+            pltpu.VMEM((2, frames + 7, 2, HALF, 4096), half16),
+            pltpu.VMEM((2, 4, 8, 2, HALF, LANES), jnp.float32),
             pltpu.VMEM((BLOCKS * HALF, 2 * LANES), half16),
             pltpu.VMEM((count * PITCH, LANES), jnp.float32),
             pltpu.VMEM((2, count, ROWS, LANES), half16),
@@ -482,7 +498,7 @@
     n_b = beams.shape[1]
     tiles = bbuf.shape[0]
 
-    @pl.loop(0, xt.shape[0], unroll=4)
+    @pl.loop(0, xt.shape[0], unroll=8)
     def _(ch):
         uv = dot(weights[...], ct[ch], NT)
         real = uv[:512, :128] - uv[512:, 128:]
@@ -495,7 +511,7 @@
     source = lax.rem(line, 16) * 16 + line // 16
     move = one_hot(iota((256, 256), 1) == source)
 
-    @pl.loop(0, tiles // 4, unroll=2)
+    @pl.loop(0, tiles // 4, unroll=4)
     def _(four):
         for j in range(4):
             tile = four * 4 + j

time: 111 us -> 109 us (0.982)
  Pallas kernels: 108 us -> 106 us
where the time goes in v6:
time: 109 us
  Pallas kernels  106 us (97%)
  local copies, waits for them, and re-layouts  1.69 us (2%)
    pallas_call x1, Pallas kernels, channelize(): pl.pallas_call(spectra_kernel, out_shape=(pltpu.VMEM((16, 256, 512), half...  91.1 us
    pallas_call x1, Pallas kernels, products(): pl.pallas_call(functools.partial(product_kernel, 1.0 / 512.0), out_shape=...  15 us

profile of v6, /device:TPU:1, one launch (start us, length us, event | category | flops | bytes accessed | tf_op | source)
XLA Modules:
  0.0 108.6 jit_solution(1490453310257477053)
XLA Ops:
  0.6 1.7 %copy.11 = bf16[16,8,2,512]{3,1,2,0:T(8,128)(2,1)} copy(bf16[16,8,2,512]{3,2,1,0:T(2,128)(2,1)} %bitcast.8) | data formatting | bytes 524288
  2.3 91.1 %spectra.1 = (bf16[16,256,512]{2,1,0:T(8,128)(2,1)S(1)}, bf16[16,256,512]{2,1,0:T(8,128)(2,1)S(1)}, bf16[1024,512]{1,0:T(8,128)(2,1)S(1)}, bf16[512,512]{1,0:T(8,128)(2,1)S(1)}) custom-call(bf16[2,32,65536]{2,1,0:T(8,128)(2,1)} %volt.1, bf16[128,1024]{1,0:T(8,128)(2,1)} %bitcast.7, f32[4,4096]{1,0:T(4,128)} %taps.1, f32[2,32,128]{2,1,0:T(8,128)} %constant.4.clone.tw, ...), custom_call_target="tpu_custom_call" | custom-call | tf_op jit(solution)/shard_map/spectra/pallas_call | solution.py:446
  93.5 15.0 %products.1 = (f32[2,4,512,512]{3,2,1,0:T(8,128)}, bf16[2,500,16,128]{3,2,1,0:T(8,128)(2,1)}) custom-call(bf16[16,256,512]{2,1,0:T(8,128)(2,1)S(1)} %get-tuple-element.8.xt, bf16[16,256,512]{2,1,0:T(8,128)(2,1)S(1)} %get-tuple-element.9.ct, bf16[1024,512]{1,0:T(8,128)(2,1)S(1)} %get-tuple-element.10.weights, bf16[512,512]{1,0:T(8,128)(2,1)S(1)} %get-tuple-element.11.order), custom_call_target="tpu_custom_call" | custom-call | tf_op jit(solution)/shard_map/products/pallas_call | solution.py:556

commit v7 on v6

--- a/solution.py
+++ b/solution.py
@@ -87,7 +87,7 @@
     volt, steer, taps, tw, lines, bands, smap, beam, calib,
     xt, ct, weights, order,
     vbuf, stage, ybuf, tbuf, sbuf, rbuf, xin, res, ebuf, gains, table, wpart, wall, mat, bidx,
-    pick,
+    pick, shares,
     load_sems, send_sems, recv_sems, steer_sems,
 ):
     me_c = lax.axis_index("chan")
@@ -149,7 +149,10 @@
     bidx[:, : beam.shape[1]] = beam[...]
 
     def share_table():
-        share = steer.at[:, pl.ds(pl.multiple_of(mine * LANES, LANES), LANES)]
+        for part in range(2):
+            for j in range(4):
+                shares[part * 4 + j] = steer[:, part, j * LANES : (j + 1) * LANES]
+        share = shares.at[mine]
 
         @pl.loop(1, n_s)
         def _(step):
@@ -451,7 +454,7 @@
             pltpu.VMEM((1024, 512), half16),
             pltpu.VMEM((512, 512), half16),
         ),
-        in_specs=[hbm] * 2 + [vmem] * 7,
+        in_specs=[hbm] + [vmem] * 8,
         out_specs=(vmem,) * 4,
         scratch_shapes=[
             pltpu.VMEM((2, frames + 7, 2, HALF, 4096), half16),
@@ -470,6 +473,7 @@
             pltpu.VMEM((LANES, 2 * LANES), half16),
             pltpu.VMEM((1, 512), jnp.int32),
             pltpu.VMEM((512, 1024), half16),
+            pltpu.VMEM((8, LANES, LANES), half16),
             pltpu.SemaphoreType.DMA((2, 2)),
             pltpu.SemaphoreType.DMA((2, 2)),
             pltpu.SemaphoreType.DMA((2, 2)),
@@ -481,7 +485,7 @@
         name="spectra",
     )(
         voltages,
-        steer.reshape(LANES, 1024),
+        steer,
         fir_taps,
         jnp.asarray(twiddles()),
         jnp.asarray(lane_table()),

time: 109 us -> 107 us (0.982)
  local copies, waits for them, and re-layouts: 1.69 us -> 0 us
    unnamed x1 -> x0, local copies, waits for them, and re-layouts: 1.69 us -> none
where the time goes in v7:
time: 107 us
  Pallas kernels  106 us (99%)
    pallas_call x1, Pallas kernels, channelize(): pl.pallas_call(spectra_kernel, out_shape=(pltpu.VMEM((16, 256, 512), half...  91.4 us
    pallas_call x1, Pallas kernels, products(): pl.pallas_call(functools.partial(product_kernel, 1.0 / 512.0), out_shape=...  15 us

profile of v7, /device:TPU:1, one launch (start us, length us, event | category | flops | bytes accessed | tf_op | source)
XLA Modules:
  0.0 107.2 jit_solution(18344293684695653818)
XLA Ops:
  0.6 91.4 %spectra.1 = (bf16[16,256,512]{2,1,0:T(8,128)(2,1)S(1)}, bf16[16,256,512]{2,1,0:T(8,128)(2,1)S(1)}, bf16[1024,512]{1,0:T(8,128)(2,1)S(1)}, bf16[512,512]{1,0:T(8,128)(2,1)S(1)}) custom-call(bf16[2,32,65536]{2,1,0:T(8,128)(2,1)} %volt.1, bf16[128,2,512]{2,1,0:T(2,128)(2,1)} %steer.1, f32[4,4096]{1,0:T(4,128)} %taps.1, f32[2,32,128]{2,1,0:T(8,128)} %constant.4.clone.tw, ...), custom_call_target="tpu_custom_call" | custom-call | tf_op jit(solution)/shard_map/spectra/pallas_call | solution.py:449
  92.0 15.0 %products.1 = (f32[2,4,512,512]{3,2,1,0:T(8,128)}, bf16[2,500,16,128]{3,2,1,0:T(8,128)(2,1)}) custom-call(bf16[16,256,512]{2,1,0:T(8,128)(2,1)S(1)} %get-tuple-element.8.xt, bf16[16,256,512]{2,1,0:T(8,128)(2,1)S(1)} %get-tuple-element.9.ct, bf16[1024,512]{1,0:T(8,128)(2,1)S(1)} %get-tuple-element.10.weights, bf16[512,512]{1,0:T(8,128)(2,1)S(1)} %get-tuple-element.11.order), custom_call_target="tpu_custom_call" | custom-call | tf_op jit(solution)/shard_map/products/pallas_call | solution.py:560
